TPU v7x, 128 devices: a whole 4x4x4 slice. The times are simulated.
128 devices in a mesh: dp: 8 (over x_lo, z), tensor: 16 (over x_hi, y, core).
Axes of the slice: x: 4 (x_hi: 2, x_lo: 2; x = x_hi * 2 + x_lo), y: 4, z: 4, core: 2. Of those that a mesh axis runs over, the one named last changes fastest.
Arguments:
- inputs: bfloat16 [4, 512, 8192], P(None, 'dp'), may hold values from -6 to 6
- norm_gain: float32 [8192], replicated, may hold values from 0.5 to 1.5
- w_query: bfloat16 [8192, 4096], P(None, 'tensor'), may hold values from -0.0625 to 0.0625
- w_kv: bfloat16 [8192, 4096], P(None, 'tensor'), may hold values from -1 to 1, as said below
- w_out: bfloat16 [4096, 8192], P('tensor'), may hold values from -0.09375 to 0.09375
- kv_cache: bfloat16 [512, 16, 256, 256], P('dp', 'tensor'), may hold values from -420 to 420, as said below
- kv_lengths: int32 [512], P('dp'), may hold values from 1 to 256, 81920 in all
- reuse_dist: int32 [8], replicated, may hold values from 1 to 64, as said below
- shard_map: int32 [16], replicated, may hold values from 0 to 15, each once
- holder_weights: bfloat16 [8, 8192, 4096], P(None, ('dp', 'tensor')), may hold values from -0.29882812 to 0.29882812
Outputs:
- outputs: bfloat16 [4, 512, 8192], P(None, 'dp')
- next_weights: bfloat16 [8192, 4096], P(None, 'tensor')
Inputs may be any that keep to these rules, and one draw needn't show every extreme that they name: `w_kv`: columns of ranks t and u are equal when t // 4 == u // 4. `kv_cache`: blocks of ranks t and u are equal when t // 4 == u // 4. `reuse_dist`: the distances are distinct.
All inputs are finite; a program needn't handle non-finite values. No bound on the sum of `kv_lengths` on one device may be relied on, other than what follows from the above.
Results may differ from a plain program's by a relative error of at most 0.011.
Values may be sent and summed in bfloat16 or wider, within the bound.
A program may use at most 128 MiB of HBM per device.

v0:
```python
import math

import jax
import jax.numpy as jnp
from jax import lax
from jax.sharding import PartitionSpec as P

HD = 128


def rotate(vec, pos):
    half = vec.shape[-1] // 2
    expo = jnp.arange(half, dtype=jnp.float32) * (2.0 / vec.shape[-1])
    inverse = jnp.float32(1000000.0) ** (-expo)
    angle = pos[:, None] * inverse[None, :]
    cosine = jnp.cos(angle)[:, None, :]
    sine = jnp.sin(angle)[:, None, :]
    low = vec[..., :half]
    high = vec[..., half:]
    return jnp.concatenate([low * cosine - high * sine, high * cosine + low * sine], axis=-1)


def on_device(
    inputs,
    norm_gain,
    w_query,
    w_kv,
    w_out,
    kv_cache,
    kv_lengths,
    reuse_dist,
    shard_map,
    holder_weights,
):
    ranks = lax.axis_size("tensor")
    chosen = jnp.argmin(reuse_dist)
    picked = lax.dynamic_index_in_dim(holder_weights, chosen, 0, keepdims=False)
    slab = picked.shape[0]
    width = picked.shape[1] // ranks
    ordered = jnp.take(picked.reshape(slab, ranks, width), shard_map, axis=1)
    served = lax.all_to_all(ordered, "tensor", split_axis=1, concat_axis=0, tiled=True)
    next_weights = lax.all_gather(served.reshape(slab * ranks, width), "dp", axis=0, tiled=True)
    steps = inputs.shape[0]
    rows = inputs.shape[1]
    heads_dev = w_query.shape[1] // HD
    scale = 1.0 / math.sqrt(HD)
    cache = kv_cache[:, 0]
    cache_keys = cache[..., :HD]
    cache_vals = cache[..., HD:]
    valid = jnp.arange(cache.shape[1], dtype=jnp.int32)[None, :] < kv_lengths[:, None]
    new_keys = jnp.zeros((rows, steps, HD), jnp.bfloat16)
    new_vals = jnp.zeros((rows, steps, HD), jnp.bfloat16)
    results = []
    for step in range(steps):
        xs = inputs[step].astype(jnp.float32)
        normed = (
            xs * lax.rsqrt(jnp.mean(xs * xs, axis=-1, keepdims=True) + 1e-06) * norm_gain
        ).astype(jnp.bfloat16)
        query = jnp.dot(normed, w_query, preferred_element_type=jnp.float32).reshape(
            rows, heads_dev, HD
        )
        pair = jnp.dot(normed, w_kv, preferred_element_type=jnp.float32)
        pos = (kv_lengths + step).astype(jnp.float32)
        query = rotate(query, pos).astype(jnp.bfloat16)
        key_now = rotate(pair[:, None, :HD], pos)[:, 0].astype(jnp.bfloat16)
        new_keys = new_keys.at[:, step].set(key_now)
        new_vals = new_vals.at[:, step].set(pair[:, HD:].astype(jnp.bfloat16))
        cache_scores = (
            jnp.einsum("rhd,rcd->rhc", query, cache_keys, preferred_element_type=jnp.float32)
            * scale
        )
        cache_scores = jnp.where(valid[:, None, :], cache_scores, -jnp.inf)
        fresh_scores = (
            jnp.einsum("rhd,rjd->rhj", query, new_keys, preferred_element_type=jnp.float32) * scale
        )
        fresh_mask = jnp.arange(steps) <= step
        fresh_scores = jnp.where(fresh_mask[None, None, :], fresh_scores, -jnp.inf)
        top = jnp.maximum(jnp.max(cache_scores, axis=-1), jnp.max(fresh_scores, axis=-1))[..., None]
        cache_exp = jnp.exp(cache_scores - top)
        fresh_exp = jnp.exp(fresh_scores - top)
        total = jnp.sum(cache_exp, axis=-1, keepdims=True) + jnp.sum(
            fresh_exp, axis=-1, keepdims=True
        )
        cache_w = (cache_exp / total).astype(jnp.bfloat16)
        fresh_w = (fresh_exp / total).astype(jnp.bfloat16)
        mixed = jnp.einsum("rhc,rcd->rhd", cache_w, cache_vals, preferred_element_type=jnp.float32)
        mixed = mixed + jnp.einsum(
            "rhj,rjd->rhd", fresh_w, new_vals, preferred_element_type=jnp.float32
        )
        attended = mixed.astype(jnp.bfloat16).reshape(rows, heads_dev * HD)
        partial_value = jnp.dot(attended, w_out, preferred_element_type=jnp.float32)
        summed = lax.psum(partial_value, "tensor")
        results.append((xs + summed).astype(jnp.bfloat16))
    return (jnp.stack(results), next_weights)


def solution(mesh):
    in_specs = (
        P(None, "dp", None),
        P(),
        P(None, "tensor"),
        P(None, "tensor"),
        P("tensor", None),
        P("dp", "tensor", None, None),
        P("dp"),
        P(),
        P(),
        P(None, ("dp", "tensor"), None),
    )
    out_specs = (P(None, "dp", None), P(None, "tensor"))
    return jax.shard_map(
        on_device, mesh=mesh, in_specs=in_specs, out_specs=out_specs, check_vma=False
    )
```

profile of v0, /device:TPU:1, one launch (start us, length us, event | category | flops | bytes accessed | tf_op | source)
XLA Modules:
  0.0 274.5 jit_solution(16931898674711808930)
XLA Ops:
  8.0 0.7 compare_select_fusion
  8.7 0.7 compare_and_fusion
  9.4 0.7 iota_reduce_fusion
  12.0 1.1 constant_dynamic-slice_fusion
  13.3 0.6 gather_fusion
  13.9 0.9 select_bitcast_fusion
  14.8 8.4 %all-to-all-start = ((bf16[64,16,256]{2,0,1:T(8,128)(2,1)}), bf16[64,16,256]{2,0,1:T(8,128)(2,1)S(1)}, u32[]{:S(2)}, u32[]{:S(2)}) async-start(bf16[64,16,256]{2,0,1:T(8,128)(2,1)} %select_bitcast_fusion), calls=%async_computation | async-start | bytes 1048576 | tf_op jit(solution)/shard_map/all_to_all | solution.py:41
  23.5 3.3 %fusion.46 = (f32[64]{0:T(128)S(1)}, f32[64]{0:T(128)S(1)}, f32[64]{0:T(128)S(1)}, f32[64]{0:T(128)S(1)}) fusion(bf16[4,64,8192]{2,1,0:T(8,128)(2,1)} %param.26), kind=kLoop, calls=%fused_computation.56 | loop fusion | flops 6291200 | bytes 4195328 | tf_op jit(solution)/shard_map/reduce_sum | solution.py:57
  26.8 2.1 fusion.126
  28.9 6.3 %copy.73 = bf16[256,8192]{1,0:T(8,128)(2,1)} copy(bf16[256,8192]{0,1:T(8,128)(2,1)} %bitcast.167) | data formatting | bytes 8388608 | tf_op jit(solution)/shard_map/dot_general | solution.py:59
  35.3 4.1 %fusion.123 = f32[64,2,128]{2,0,1:T(8,128)S(1)} fusion(bf16[2,128,8192]{2,1,0:T(8,128)(2,1)} %bitcast.163, f32[8192]{0:T(1024)S(1)} %copy-done.9, f32[64]{0:T(128)S(1)} %get-tuple-element.169, bf16[4,64,8192]{2,1,0:T(8,128)(2,1)} %param.26), kind=kOutput, calls=%fused_computation.99 | convolution fusion | flops 270532608 | bytes 5341440 | tf_op jit(solution)/shard_map/dot_general | solution.py:59
  39.4 2.3 fusion.120
  41.7 2.8 %fusion.117 = f32[64,2,128]{2,0,1:T(8,128)S(1)} fusion(bf16[2,128,8192]{2,1,0:T(8,128)(2,1)S(1)} %bitcast.164, f32[64]{0:T(128)S(1)} %get-tuple-element.168, f32[8192]{0:T(1024)S(1)} %copy-done.9, bf16[4,64,8192]{2,1,0:T(8,128)(2,1)} %param.26), kind=kOutput, calls=%fused_computation.95 | convolution fusion | flops 270532608 | bytes 5341440 | tf_op jit(solution)/shard_map/dot_general | solution.py:59
  44.5 0.9 fusion.114
  45.4 1.4 fusion.111
  47.0 0.5 multiply_cosine_fusion.7
  47.8 0.3 fusion.257
  48.1 1.3 fusion.256
  49.4 0.2 fusion.195
  49.9 0.9 fusion.108
  51.0 1.3 fusion.254
  52.3 0.5 fusion.200
  52.9 0.3 fusion.255
  54.0 0.8 copy-done.10
  55.0 0.3 fusion.253
  55.3 3.6 %fusion.252 = (f32[64,2]{1,0:T(8,128)S(1)}, f32[64,2,256]{2,1,0:T(2,128)S(1)}) fusion(bf16[64,256,256]{2,1,0:T(8,128)(2,1)} %bitcast.175, bf16[64,2,128]{2,0,1:T(8,128)(2,1)S(1)} %pad_maximum_fusion.3, pred[64,256]{1,0:T(8,128)(4,1)S(1)} %iota_compare_fusion.1), kind=kOutput, calls=%fused_computation.301 | convolution fusion | flops 8486784 | bytes 4375040 | tf_op jit(solution)/shard_map/rhd,rcd->rhc/dot_general | solution.py:69
  59.6 2.8 %fusion.105 = f32[64,2,128]{2,0,1:T(8,128)S(1)} fusion(bf16[2,128,8192]{2,1,0:T(8,128)(2,1)S(1)} %bitcast.166, f32[64]{0:T(128)S(1)} %get-tuple-element.166, f32[8192]{0:T(1024)S(1)} %copy-done.9, bf16[4,64,8192]{2,1,0:T(8,128)(2,1)} %param.26), kind=kOutput, calls=%fused_computation.87 | convolution fusion | flops 270532608 | bytes 5341440 | tf_op jit(solution)/shard_map/dot_general | solution.py:59
  62.6 0.3 fusion.251
  62.9 3.6 %fusion.250 = (f32[64,2]{1,0:T(8,128)S(1)}, f32[64,2,256]{2,1,0:T(2,128)S(1)}) fusion(bf16[64,256,256]{2,1,0:T(8,128)(2,1)} %bitcast.176, bf16[64,2,128]{2,0,1:T(8,128)(2,1)S(1)} %pad_maximum_fusion.4, pred[64,256]{1,0:T(8,128)(4,1)S(1)} %iota_compare_fusion.1), kind=kOutput, calls=%fused_computation.299 | convolution fusion | flops 8486784 | bytes 4375040 | tf_op jit(solution)/shard_map/rhd,rcd->rhc/dot_general | solution.py:69
  67.0 0.3 fusion.176
  67.3 0.3 fusion.173
  67.7 0.3 fusion.170
  68.0 0.3 fusion.167
  68.4 0.7 fusion.101
  69.1 1.1 copy-done.4
  70.2 2.2 fusion.224
  72.4 0.7 fusion.98
  73.1 2.2 fusion.221
  75.3 0.7 fusion.95
  76.0 2.2 fusion.218
  78.2 0.7 fusion.92
  78.9 2.2 fusion.215
  81.1 28.6 %all-gather.2.cloned.1.call-done = bf16[8192,256]{1,0:T(8,128)(2,1)} async-done(((bf16[1024,256]{1,0:T(8,128)(2,1)}), bf16[8192,256]{1,0:T(8,128)(2,1)}) %all-gather.2.cloned.1.call-update) | async-done | bytes 4194320 | tf_op jit(solution)/shard_map/all_gather | solution.py:42
  109.7 145.8 %all-reduce.5.cloned.1.call-done = (f32[64,8192]{1,0:T(8,128)}, f32[64,8192]{1,0:T(8,128)}, f32[64,8192]{1,0:T(8,128)}, f32[64,8192]{1,0:T(8,128)}) async-done(((f32[64,8192]{1,0:T(8,128)}, f32[64,8192]{1,0:T(8,128)}, f32[64,8192]{1,0:T(8,128)}, f32[64,8192]{1,0:T(8,128)}), (f32[64,8192]{1,0:T(8,128)}, f32[64,8192]{1,0:T(8,128)}, f32[64,8192]{1,0:T(8,128)}, ...) | async-done | bytes 8388624 | tf_op jit(solution)/shard_map/psum | solution.py:92
  255.6 5.7 %fusion.125 = (bf16[1,64,8192]{2,1,0:T(8,128)(2,1)S(1)}, bf16[1,64,8192]{2,1,0:T(8,128)(2,1)S(1)}, bf16[1,64,8192]{2,1,0:T(8,128)(2,1)S(1)}, bf16[1,64,8192]{2,1,0:T(8,128)(2,1)S(1)}) fusion(f32[64,8192]{1,0:T(8,128)} %get-tuple-element.107, bf16[4,64,8192]{2,1,0:T(8,128)(2,1)} %param.26, f32[64,8192]{1,0:T(8,128)} %get-tuple-element.106, ...), kind=kLoop, calls=%fused_computation.100 | loop fusion | flops 6291456 | bytes 16777216 | tf_op jit(solution)/shard_map/stack | solution.py:94
  261.3 2.4 pad_maximum_fusion
  263.8 1.3 copy-done.8
  265.0 2.0 copy.162
  (85 shorter events, 3.8 us)
Async XLA Ops:
  8.0 1.4 copy-start
  8.0 15.4 %copy-start.11 = (s32[64]{0:T(128)S(1)}, s32[64]{0:T(128)}, u32[]{:S(2)}) copy-start(s32[64]{0:T(128)} %param.32) | copy-start | bytes 772
  13.1 13.6 %copy-start.9 = (f32[8192]{0:T(1024)S(1)}, f32[8192]{0:T(1024)}, u32[]{:S(2)}) copy-start(f32[8192]{0:T(1024)} %param.27) | copy-start | bytes 98308
  14.8 39.1 %all-to-all-start = ((bf16[64,16,256]{2,0,1:T(8,128)(2,1)}), bf16[64,16,256]{2,0,1:T(8,128)(2,1)S(1)}, u32[]{:S(2)}, u32[]{:S(2)}) async-start(bf16[64,16,256]{2,0,1:T(8,128)(2,1)} %select_bitcast_fusion), calls=%async_computation | async-start | bytes 1048576 | tf_op jit(solution)/shard_map/all_to_all | solution.py:41
  23.3 86.4 %all-gather.2.cloned.1.call-start = ((), (), s32[]{:S(2)}) async-start(), calls=%async_computation.1 | async-start | bytes 4718592 | tf_op jit(solution)/shard_map/all_gather | solution.py:42
  23.3 3.5 %copy-start.5 = (bf16[8192,256]{1,0:T(8,128)(2,1)S(1)}, bf16[8192,256]{1,0:T(8,128)(2,1)}, u32[]{:S(2)}) copy-start(bf16[8192,256]{1,0:T(8,128)(2,1)} %param.29) | copy-start | bytes 12582916
  35.3 4.1 %copy-start.6 = (bf16[8192,256]{1,0:T(8,128)(2,1)S(1)}, bf16[8192,256]{1,0:T(8,128)(2,1)}, u32[]{:S(2)}) copy-start(bf16[8192,256]{1,0:T(8,128)(2,1)} %param.29) | copy-start | bytes 12582916
  35.3 6.4 %copy-start.2 = (bf16[256,8192]{1,0:T(8,128)(2,1)S(1)}, bf16[256,8192]{1,0:T(8,128)(2,1)}, u32[]{:S(2)}) copy-start(bf16[256,8192]{1,0:T(8,128)(2,1)} %copy.73) | copy-start | bytes 12582916
  39.3 5.1 %copy-start.7 = (bf16[4,64,8192]{2,1,0:T(8,128)(2,1)S(1)}, bf16[4,64,8192]{2,1,0:T(8,128)(2,1)}, u32[]{:S(2)}) copy-start(bf16[4,64,8192]{2,1,0:T(8,128)(2,1)} %param.26) | copy-start | bytes 12582916
  41.6 6.5 %slice-start = ((s8[8388608]{0:T(1024)(128)(4,1)}), s8[4194304]{0:T(1024)(128)(4,1)S(1)}, s32[]{:S(2)}) async-start(s8[8388608]{0:T(1024)(128)(4,1)} %bitcast.177), calls=%async_computation.3 | async-start | bytes 8388608
  44.5 3.6 %slice-start.1 = ((s8[8388608]{0:T(1024)(128)(4,1)}), s8[4194304]{0:T(1024)(128)(4,1)S(1)}, s32[]{:S(2)}) async-start(s8[8388608]{0:T(1024)(128)(4,1)} %bitcast.177), calls=%async_computation.4 | async-start | bytes 8388608
  54.0 0.8 copy-start.10
  54.8 200.8 %all-reduce.5.cloned.1.call-start = ((), (), s32[]{:S(2)}) async-start(), calls=%async_computation.2 | async-start | bytes 16777216 | tf_op jit(solution)/shard_map/psum | solution.py:92
  55.0 4.5 %copy-start.3 = (bf16[256,8192]{1,0:T(8,128)(2,1)S(1)}, bf16[256,8192]{1,0:T(8,128)(2,1)}, u32[]{:S(2)}) copy-start(bf16[256,8192]{1,0:T(8,128)(2,1)} %copy.73) | copy-start | bytes 12582916
  59.6 8.8 %slice-start.2 = ((s8[8388608]{0:T(1024)(128)(4,1)}), s8[4194304]{0:T(1024)(128)(4,1)S(1)}, s32[]{:S(2)}) async-start(s8[8388608]{0:T(1024)(128)(4,1)} %bitcast.181), calls=%async_computation.5 | async-start | bytes 8388608
  62.9 5.5 %slice-start.3 = ((s8[8388608]{0:T(1024)(128)(4,1)}), s8[4194304]{0:T(1024)(128)(4,1)S(1)}, s32[]{:S(2)}) async-start(s8[8388608]{0:T(1024)(128)(4,1)} %bitcast.181), calls=%async_computation.6 | async-start | bytes 8388608
  68.0 2.2 copy-start.4
  261.3 3.7 %copy-start.8 = (bf16[8192,256]{1,0:T(8,128)(2,1)S(1)}, bf16[8192,256]{1,0:T(8,128)(2,1)}, u32[]{:S(2)}) copy-start(bf16[8192,256]{1,0:T(8,128)(2,1)} %all-gather.2.cloned.1.call-done) | copy-start | bytes 12582916
  261.3 5.7 %copy-start.1 = (s32[8]{0:T(128)S(1)}, s32[8]{0:T(128)}, u32[]{:S(2)}) copy-start(s32[8]{0:T(128)} %param.33) | copy-start | bytes 100
Sparse Core Ops, SparseCore 0:
  54.9 54.7 all-gather.1
Sparse Core Ops, SparseCore 1:
  81.2 174.3 all-reduce.4
where the time goes:
time: 276 us; the launch traced here: 274 us
  waiting for transfers between devices  174 us (63%)
  matrix products  41.1 us (15%)
  other arithmetic  18.6 us (7%)
  between operations  18 us (7%)
  local copies, waits for them, and re-layouts  13.6 us (5%)
  starting transfers between devices  8.71 us (3%)
    psum x1, waiting for transfers between devices, on_device(): summed = lax.psum(partial_value, 'tensor')  146 us
    all_gather x1, waiting for transfers between devices, on_device(): lax.all_gather(served.reshape(slab * ranks, width), 'dp', axis=0, tiled=T...  28.6 us
    dot_general x4, matrix products, on_device(): jnp.dot(normed, w_query, preferred_element_type=jnp.float32)  11.1 us
    dot_general x4, matrix products, on_device(): jnp.einsum('rhd,rcd->rhc', query, cache_keys, preferred_element_type=jnp....  9.76 us
    dot_general x4, matrix products, on_device(): partial_value = jnp.dot(attended, w_out, preferred_element_type=jnp.float32)  8.75 us
    all_to_all x1, starting transfers between devices, on_device(): lax.all_to_all(ordered, 'tensor', split_axis=1, concat_axis=0, tiled=True)  8.45 us
    another operation x2, other arithmetic, on_device(): return (jnp.stack(results), next_weights)  8.17 us
    dot_general x1, local copies, waits for them, and re-layouts, on_device(): jnp.dot(normed, w_query, preferred_element_type=jnp.float32)  6.33 us
  transfers between devices with their start and end apart: 3, of which 2 were waited for; matrix products, arithmetic and copies ran while one was open for 20% of the time, Pallas kernels for 0%

commit v1 on v0

v1 whole, which is shorter than its diff:
```python
import functools
import math

import jax
import jax.numpy as jnp
import numpy as np
from jax import lax
from jax.experimental import pallas as pl
from jax.experimental.pallas import tpu as pltpu
from jax.sharding import PartitionSpec as P

MESH = pl.DeviceIdType.MESH
HD = 128
STEPS = 4
ROWS = 64
HALF = 32
WIDTH = 8192
CHUNK = 1024
NCHUNK = WIDTH // CHUNK
COLS = 4096
CTX = 256
NCOPY = 96
BF = jnp.bfloat16
F32 = jnp.float32


def mult(value, by):
    return pl.multiple_of(value, by)


def kernel(
    x_hbm, gain, wq_hbm, wkv_hbm, wo_hbm, kv_hbm, len_v, dist, smap, hold_hbm, inverse,
    out, nw,
    xv, w, wo, kv, hold, ordr, w1r, acc, sq, ybf, cs, sn, qs, qr, kn, vn, qf, sc, fs, pw, pf, mix,
    att, part, ra, rax, rbx, rb, sa, sb, keep_a, keep_b,
    ld, chunk_sem, hold_sem, ssem, rsem,
):
    dp = lax.axis_index("dp")
    tensor = lax.axis_index("tensor")
    xl, z = dp // 4, lax.rem(dp, 4)
    xh, y, c = tensor // 8, lax.rem(tensor // 2, 4), lax.rem(tensor, 2)

    def dev(xl_, xh_, y_, z_, c_):
        return (xl_ * 4 + z_, xh_ * 8 + y_ * 2 + c_)

    def ring(value, by):
        return lax.rem(value + by + 4, 4)

    copies = []

    def send(src, dst, where):
        i = len(copies)
        cp = pltpu.make_async_remote_copy(
            src_ref=src, dst_ref=dst, send_sem=ssem.at[i], recv_sem=rsem.at[i],
            device_id=where, device_id_type=MESH,
        )
        cp.start()
        copies.append([cp, False])
        return i

    def arrived(i):
        copies[i][0].wait_recv()
        copies[i][1] = True

    sibling = dev(xl, xh, y, z, 1 - c)
    across = dev(xl, 1 - xh, y, z, c)
    cross = dev(1 - xl, 1 - xh, y, z, c)
    near = dev(1 - xl, xh, y, z, c)
    z_up = dev(xl, xh, y, ring(z, 1), c)
    z_down = dev(xl, xh, y, ring(z, -1), c)

    def same_core(k):
        return dev(xl, xh, ring(y, k), z, c)

    def hold_load(t):
        cols = pl.ds(mult(t * 256, 256), 256)
        return pltpu.make_async_copy(hold_hbm.at[:, :, cols], hold.at[:, t], hold_sem.at[t])

    def start_hold(t, carry):
        hold_load(t).start()
        return carry

    lax.fori_loop(0, 16, start_hold, 0)

    def chunk_loads(i):
        ks = pl.ds(mult(i * CHUNK, CHUNK), CHUNK)
        return (
            pltpu.make_async_copy(x_hbm.at[:, :, ks], xv.at[:, :, ks], chunk_sem.at[i, 0]),
            pltpu.make_async_copy(wq_hbm.at[ks], w.at[ks, pl.ds(0, 256)], chunk_sem.at[i, 1]),
            pltpu.make_async_copy(wkv_hbm.at[ks], w.at[ks, pl.ds(256, 256)], chunk_sem.at[i, 2]),
        )

    def start_chunk(i, carry):
        for cp in chunk_loads(i):
            cp.start()
        return carry

    lax.fori_loop(0, NCHUNK, start_chunk, 0)
    my_half = pl.ds(mult(c * HALF, HALF), HALF)
    load_kv = pltpu.make_async_copy(kv_hbm.at[my_half, 0], kv, ld.at[1])
    load_kv.start()
    my_cols = pl.ds(mult(c * COLS, COLS), COLS)
    sib_cols = pl.ds(mult((1 - c) * COLS, COLS), COLS)
    my_wo = pl.ds(mult(c * 256, 256), 256)
    load_wo = pltpu.make_async_copy(wo_hbm.at[:, my_cols], wo.at[my_wo], ld.at[2])
    load_wo.start()

    barrier = pltpu.get_barrier_semaphore()
    greet = [sibling, across, cross, near, z_up, z_down]
    for k in (1, 2, 3):
        for other in (c, 1 - c):
            greet.append(dev(xl, xh, ring(y, k), z, other))
    for where in greet:
        pl.semaphore_signal(barrier, inc=1, device_id=where, device_id_type=MESH)

    lengths = len_v[...].astype(F32)
    eye = lax.broadcasted_iota(jnp.int32, (ROWS, ROWS), 0) == lax.broadcasted_iota(
        jnp.int32, (ROWS, ROWS), 1
    )
    position = jnp.sum(jnp.where(eye, lengths, 0.0), axis=1, keepdims=True)
    sign = jnp.where(lax.broadcasted_iota(jnp.int32, (1, HD), 1) < HD // 2, -1.0, 1.0)
    for s in range(STEPS):
        angle = (position + float(s)) * inverse[...]
        cs[s] = jnp.cos(angle)
        sn[s] = jnp.sin(angle) * sign
    acc[...] = jnp.zeros_like(acc)
    sq[...] = jnp.zeros_like(sq)

    best = dist[0] * 8
    for i in range(1, 8):
        best = jnp.minimum(best, dist[i] * 8 + i)
    chosen = lax.rem(best, 8)

    def hold_done(t, carry):
        hold_load(t).wait()
        return carry

    def order(t, carry):
        ordr[t] = hold[chosen, smap[t]]
        return carry

    lax.fori_loop(0, 16, hold_done, 0)
    lax.fori_loop(0, 16, order, 0)

    pl.semaphore_wait(barrier, len(greet))

    def rows_of(xl_, xh_, y_, z_, c_):
        return pl.ds(mult(((xl_ * 4 + z_) * 16 + xh_ * 8 + y_ * 2 + c_) * 64, 64), 64)

    def slab_of(xl_, xh_, z_):
        return pl.ds(mult(((xl_ * 4 + z_) * 16 + xh_ * 8) * 64, 512), 512)

    cross_copy = send(ordr.at[pl.ds(mult((1 - xh) * 8, 8), 8)], w1r, cross)
    mine = rows_of(xl, xh, y, z, c)
    own_copies = []
    for k in (2, 1, 3, 0):
        for flip in (0, 1):
            if k == 0 and flip == 0:
                continue
            yk = ring(y, k)
            ck = (c, 1 - c)[flip]
            own_copies.append(
                send(ordr.at[xh * 8 + yk * 2 + ck], nw.at[mine], dev(xl, xh, yk, z, ck))
            )
    nw[mine] = ordr[xh * 8 + y * 2 + c]
    wo_copy = send(wo_hbm.at[:, sib_cols], wo.at[my_wo], sibling)

    def project(i, carry):
        ks = pl.ds(mult(i * CHUNK, CHUNK), CHUNK)
        for cp in chunk_loads(i):
            cp.wait()
        g = gain[:, ks]
        for s in range(STEPS):
            xs = xv[s, :, ks].astype(F32)
            ybf[s] = (xs * g).astype(BF)
            xx = xs * xs
            total = xx[:, 0:128]
            for j in range(1, CHUNK // 128):
                total = total + xx[:, j * 128:(j + 1) * 128]
            sq[s] += total
        acc[...] += jnp.dot(
            ybf[...].reshape(STEPS * ROWS, CHUNK), w[ks, :], preferred_element_type=F32
        )
        return carry

    lax.fori_loop(0, NCHUNK, project, 0)

    def turn(v, s):
        return v * cs[s] + pltpu.roll(v, HD // 2, 1) * sn[s]

    for s in range(STEPS):
        scale = lax.rsqrt(jnp.sum(sq[s], axis=1, keepdims=True) * (1.0 / WIDTH) + 1e-06)
        block = pl.ds(s * ROWS, ROWS)
        for h in range(2):
            cols = slice(h * HD, (h + 1) * HD)
            qs[s, :, cols] = turn(acc[block, cols] * scale, s).astype(BF)
        kn[s] = turn(acc[block, 256:384] * scale, s).astype(BF)
        vn[s] = (acc[block, 384:512] * scale).astype(BF)

    sib_half = pl.ds(mult((1 - c) * HALF, HALF), HALF)
    q_copy = send(qs.at[:, sib_half, :], qr, sibling)

    arrived(cross_copy)
    theirs = rows_of(1 - xl, 1 - xh, y, z, c)
    cross_copies = []
    for k in (2, 1, 3, 0):
        for flip in (0, 1):
            if k == 0 and flip == 0:
                continue
            yk = ring(y, k)
            ck = (c, 1 - c)[flip]
            cross_copies.append(
                send(w1r.at[yk * 2 + ck], nw.at[theirs], dev(xl, xh, yk, z, ck))
            )
    nw[theirs] = w1r[y * 2 + c]

    def around(slab):
        return send(nw.at[slab], nw.at[slab], z_up), send(nw.at[slab], nw.at[slab], z_down)

    for i in own_copies:
        arrived(i)
    slab_0a = slab_of(xl, xh, z)
    z_0a = around(slab_0a)
    near_a = send(nw.at[slab_0a], nw.at[slab_0a], near)

    for s in range(STEPS):
        for h in range(2):
            qf[pl.ds(s * 2 + h, HALF, stride=16), :] = qs[s, my_half, h * HD:(h + 1) * HD].astype(
                F32
            )
    arrived(q_copy)
    for s in range(STEPS):
        for h in range(2):
            qf[pl.ds(8 + s * 2 + h, HALF, stride=16), :] = qr[s, :, h * HD:(h + 1) * HD].astype(F32)
    load_kv.wait()

    def score(r, carry):
        rows = pl.ds(mult(r * 16, 16), 16)
        sc[rows, :] = lax.dot_general(
            qf[rows, :].astype(BF), kv[r, :, 0:HD], (((1,), (1,)), ((), ())),
            preferred_element_type=F32,
        )
        return carry

    lax.fori_loop(0, HALF, score, 0, unroll=4)
    keys = kn[:, my_half, :].reshape(STEPS * HALF, HD)
    fs[...] = lax.dot_general(
        qf[...].astype(BF), keys, (((1,), (1,)), ((), ())), preferred_element_type=F32
    )

    for i in cross_copies:
        arrived(i)
    slab_0b = slab_of(1 - xl, 1 - xh, z)
    z_0b = around(slab_0b)
    near_b = send(nw.at[slab_0b], nw.at[slab_0b], near)

    factor = 1.0 / math.sqrt(HD)
    neg = -jnp.inf

    def soften(b, carry):
        rows = pl.ds(mult(b * 64, 64), 64)
        i = lax.broadcasted_iota(jnp.int32, (64, 1), 0) + b * 64
        r = i >> 4
        step = (i & 7) >> 1
        lane = lax.broadcasted_iota(jnp.int32, (1, ROWS), 1)
        limit = jnp.sum(jnp.where(lane == r + c * HALF, lengths, 0.0), axis=1, keepdims=True)
        place = lax.broadcasted_iota(jnp.int32, (1, CTX), 1).astype(F32)
        cached = jnp.where(place < limit, sc[rows, :] * factor, neg)
        n = lax.broadcasted_iota(jnp.int32, (1, 128), 1)
        usable = ((n & 31) == r) & ((n >> 5) <= step)
        fresh = jnp.where(usable, fs[rows, :] * factor, neg)
        top = jnp.maximum(
            jnp.max(cached, axis=1, keepdims=True), jnp.max(fresh, axis=1, keepdims=True)
        )
        ce = jnp.exp(cached - top)
        fe = jnp.exp(fresh - top)
        total = jnp.sum(ce, axis=1, keepdims=True) + jnp.sum(fe, axis=1, keepdims=True)
        share = 1.0 / total
        pw[rows, :] = (ce * share).astype(BF)
        pf[rows, :] = (fe * share).astype(BF)
        return carry

    lax.fori_loop(0, 8, soften, 0)

    values = vn[:, my_half, :].reshape(STEPS * HALF, HD)
    mix[...] = jnp.dot(pf[...], values, preferred_element_type=F32)

    def weigh(r, carry):
        rows = pl.ds(mult(r * 16, 16), 16)
        mix[rows, :] += jnp.dot(pw[rows, :], kv[r, :, HD:2 * HD], preferred_element_type=F32)
        return carry

    lax.fori_loop(0, HALF, weigh, 0, unroll=4)
    for source in range(2):
        for s in range(STEPS):
            for h in range(2):
                base = (c if source == 0 else 1 - c) * 256 + h * HD
                att[s, my_half, pl.ds(mult(base, HD), HD)] = mix[
                    pl.ds(source * 8 + s * 2 + h, HALF, stride=16), :
                ].astype(BF)
    att_copy = send(att.at[:, my_half, :], att.at[:, my_half, :], sibling)
    load_wo.wait()
    arrived(wo_copy)
    arrived(att_copy)

    first = pl.ds(0, 2)
    second = pl.ds(2, 2)
    a_copies, b_copies = {}, {}
    attended = att[...].reshape(STEPS * ROWS, 2 * 256)
    for k in (2, 1, 3, 0):
        yk = ring(y, k)
        for flip in (1, 0):
            side = (xh, 1 - xh)[flip]
            cols = pl.ds(mult(yk * 1024 + side * 512, 512), 512)
            term = jnp.dot(attended, wo[:, cols], preferred_element_type=F32)
            part[:, :, cols] = term.astype(BF).reshape(STEPS, ROWS, 512)
            if flip == 1:
                b_copies[k] = send(part.at[second, :, cols], rbx.at[k], across)
        if k:
            cols = pl.ds(mult(yk * 1024, 1024), 1024)
            a_copies[k] = send(part.at[first, :, cols], ra.at[k - 1], same_core(k))

    slab_1a = slab_of(1 - xl, xh, z)
    slab_1b = slab_of(xl, 1 - xh, z)
    arrived(near_a)
    z_1a = around(slab_1a)
    arrived(near_b)
    z_1b = around(slab_1b)

    b2 = {}
    for k in (2, 1, 3):
        arrived(b_copies[k])
        cols = pl.ds(mult(ring(y, k) * 1024 + xh * 512, 512), 512)
        sb[k - 1] = (part[second, :, cols].astype(F32) + rbx[k].astype(F32)).astype(BF)
        b2[k] = send(sb.at[k - 1], rb.at[k - 1], same_core(k))
    for k in (1, 2, 3):
        arrived(a_copies[k])

    def own_sum(side):
        cols = pl.ds(mult(y * 1024 + side * 512, 512), 512)
        inner = pl.ds(mult(side * 512, 512), 512)
        total = part[first, :, cols].astype(F32)
        for k in (1, 2, 3):
            total = total + ra[k - 1, :, :, inner].astype(F32)
        return total

    sa[...] = own_sum(1 - xh).astype(BF)
    a2 = send(sa, rax, across)
    keep_a[...] = own_sum(xh)
    here = pl.ds(mult(y * 1024 + xh * 512, 512), 512)
    arrived(b_copies[0])
    keep_b[...] = part[second, :, here].astype(F32) + rbx[0].astype(F32)

    def onward(i, slab, where):
        arrived(i)
        return send(nw.at[slab], nw.at[slab], where)

    onward(z_0a[0], slab_of(xl, xh, ring(z, -1)), z_up)
    onward(z_0b[1], slab_of(1 - xl, 1 - xh, ring(z, 1)), z_down)

    def chunk_at(c_, y_, xh_):
        return pl.ds(mult(c_ * COLS + y_ * 1024 + xh_ * 512, 512), 512)

    def give(part_of, cols, wheres):
        ref = out.at[part_of, :, cols]
        return [send(ref, ref, where) for where in wheres]

    own = chunk_at(c, y, xh)
    spread = [across, same_core(2), same_core(1), same_core(3)]
    for k in (1, 2, 3):
        arrived(b2[k])
    total = xv[second, :, own].astype(F32) + keep_b[...]
    for k in (1, 2, 3):
        total = total + rb[k - 1].astype(F32)
    out[second, :, own] = total.astype(BF)
    gb = give(second, own, spread)
    arrived(a2)
    out[first, :, own] = (xv[first, :, own].astype(F32) + keep_a[...] + rax[...].astype(F32)).astype(
        BF
    )
    ga = give(first, own, spread)
    give(second, own, [sibling])
    give(first, own, [sibling])

    onward(z_1a[0], slab_of(1 - xl, xh, ring(z, -1)), z_up)
    onward(z_1b[1], slab_of(xl, 1 - xh, ring(z, 1)), z_down)

    last = []
    for j, k in ((2, 1), (3, 3), (1, 2)):
        arrived(gb[j])
        cols = chunk_at(c, ring(y, -k), xh)
        last.append((second, chunk_at(c, ring(y, -k), 1 - xh), give(second, cols, [across])[0]))
        give(second, cols, [sibling])
    arrived(ga[0])
    cols = chunk_at(c, y, 1 - xh)
    for k, i in zip((2, 1, 3), give(first, cols, spread[1:])):
        last.append((first, chunk_at(c, ring(y, -k), 1 - xh), i))
    give(first, cols, [sibling])
    arrived(gb[0])
    give(second, cols, [sibling])
    for j, k in ((2, 1), (3, 3), (1, 2)):
        arrived(ga[j])
        give(first, chunk_at(c, ring(y, -k), xh), [sibling])
    for part_of, cols, i in last:
        arrived(i)
        give(part_of, cols, [sibling])

    for cp, done in copies:
        if not done:
            cp.wait_recv()
        cp.wait_send()


def on_device(
    inputs, norm_gain, w_query, w_kv, w_out, kv_cache, kv_lengths, reuse_dist, shard_map,
    holder_weights,
):
    expo = np.arange(HD // 2, dtype=np.float32) * np.float32(2.0 / HD)
    inverse = np.float32(1000000.0) ** (-expo)
    inverse = jnp.asarray(np.concatenate([inverse, inverse])[None, :], F32)
    hbm = pl.BlockSpec(memory_space=pltpu.HBM)
    vmem = pl.BlockSpec(memory_space=pltpu.VMEM)
    smem = pl.BlockSpec(memory_space=pltpu.SMEM)
    dma = pltpu.SemaphoreType.DMA
    return pl.pallas_call(
        kernel,
        out_shape=(
            pltpu.VMEM((STEPS, ROWS, WIDTH), BF),
            pltpu.VMEM((WIDTH, 256), BF),
        ),
        in_specs=[hbm, vmem, hbm, hbm, hbm, hbm, vmem, smem, smem, hbm, vmem],
        out_specs=(vmem, vmem),
        scratch_shapes=[
            pltpu.VMEM((STEPS, ROWS, WIDTH), BF),
            pltpu.VMEM((WIDTH, 512), BF),
            pltpu.VMEM((512, COLS), BF),
            pltpu.VMEM((HALF, CTX, 2 * HD), BF),
            pltpu.VMEM((8, 16, 64, 256), BF),
            pltpu.VMEM((16, 64, 256), BF),
            pltpu.VMEM((8, 64, 256), BF),
            pltpu.VMEM((STEPS * ROWS, 512), F32),
            pltpu.VMEM((STEPS, ROWS, 128), F32),
            pltpu.VMEM((STEPS, ROWS, CHUNK), BF),
            pltpu.VMEM((STEPS, ROWS, HD), F32),
            pltpu.VMEM((STEPS, ROWS, HD), F32),
            pltpu.VMEM((STEPS, ROWS, 256), BF),
            pltpu.VMEM((STEPS, HALF, 256), BF),
            pltpu.VMEM((STEPS, ROWS, HD), BF),
            pltpu.VMEM((STEPS, ROWS, HD), BF),
            pltpu.VMEM((512, HD), F32),
            pltpu.VMEM((512, CTX), F32),
            pltpu.VMEM((512, 128), F32),
            pltpu.VMEM((512, CTX), BF),
            pltpu.VMEM((512, 128), BF),
            pltpu.VMEM((512, HD), F32),
            pltpu.VMEM((STEPS, ROWS, 512), BF),
            pltpu.VMEM((STEPS, ROWS, COLS), BF),
            pltpu.VMEM((3, 2, ROWS, 1024), BF),
            pltpu.VMEM((2, ROWS, 512), BF),
            pltpu.VMEM((4, 2, ROWS, 512), BF),
            pltpu.VMEM((3, 2, ROWS, 512), BF),
            pltpu.VMEM((2, ROWS, 512), BF),
            pltpu.VMEM((3, 2, ROWS, 512), BF),
            pltpu.VMEM((2, ROWS, 512), F32),
            pltpu.VMEM((2, ROWS, 512), F32),
            dma((3,)),
            dma((NCHUNK, 3)),
            dma((16,)),
            dma((NCOPY,)),
            dma((NCOPY,)),
        ],
        compiler_params=pltpu.CompilerParams(
            collective_id=0, has_side_effects=True, vmem_limit_bytes=48 * 1024 * 1024
        ),
    )(
        inputs, norm_gain.reshape(1, WIDTH), w_query, w_kv, w_out, kv_cache,
        kv_lengths.reshape(1, ROWS), reuse_dist, shard_map, holder_weights, inverse,
    )


def solution(mesh):
    in_specs = (
        P(None, "dp", None),
        P(),
        P(None, "tensor"),
        P(None, "tensor"),
        P("tensor", None),
        P("dp", "tensor", None, None),
        P("dp"),
        P(),
        P(),
        P(None, ("dp", "tensor"), None),
    )
    out_specs = (P(None, "dp", None), P(None, "tensor"))
    return jax.shard_map(
        on_device, mesh=mesh, in_specs=in_specs, out_specs=out_specs, check_vma=False
    )
```

time: 276 us -> 73 us (0.26)
  waiting for transfers between devices: 174 us -> 0 us
  Pallas kernels: 0 us -> 68.2 us
  matrix products: 41.1 us -> 0 us
  other arithmetic: 18.6 us -> 0 us
  between operations: 18 us -> 0.64 us
  local copies, waits for them, and re-layouts: 13.6 us -> 4.03 us
  starting transfers between devices: 8.71 us -> 0 us
    psum x1 -> x0, waiting for transfers between devices: 146 us -> none  [on_device(): summed = lax.psum(partial_value, 'tensor')]
    pallas_call x0 -> x1, Pallas kernels: none -> 68.2 us  [on_device(): pl.pallas_call(kernel, out_shape=(pltpu.VMEM((STEPS, ROWS, WIDTH), BF), p...]
    dot_general x28 -> x0, matrix products: 41.1 us -> none  [the longest x4 11.1 us: on_device(): jnp.dot(normed, w_query, preferred_element_type=jnp.float32)]
    all_gather x1 -> x0, waiting for transfers between devices: 28.6 us -> none  [on_device(): lax.all_gather(served.reshape(slab * ranks, width), 'dp', axis=0, tiled=T...]
    another operation x9 -> x0, other arithmetic: 9.84 us -> none  [the longest x2 8.17 us: on_device(): return (jnp.stack(results), next_weights)]
    all_to_all x1 -> x0, starting transfers between devices: 8.45 us -> none  [on_device(): lax.all_to_all(ordered, 'tensor', split_axis=1, concat_axis=0, tiled=True)]
    dot_general x1 -> x0, local copies, waits for them, and re-layouts: 6.33 us -> none  [on_device(): jnp.dot(normed, w_query, preferred_element_type=jnp.float32)]
    reduce_sum x9 -> x0, other arithmetic: 5.12 us -> none  [the longest x1 3.27 us: on_device(): jnp.mean(xs * xs, axis=-1, keepdims=True) + 1e-06]
  transfers between devices with their start and end apart: 3 -> 0, of which waited for: 2 -> 0; matrix products, arithmetic and copies ran while one was open for 20% -> 0% of each run, Pallas kernels for 0% -> 0%
where the time goes in v1:
time: 73 us; the launch traced here: 72.8 us
  Pallas kernels  68.2 us (93%)
  local copies, waits for them, and re-layouts  4.03 us (6%)
    pallas_call x1, Pallas kernels, on_device(): pl.pallas_call(kernel, out_shape=(pltpu.VMEM((STEPS, ROWS, WIDTH), BF), p...  68.2 us
    unnamed x2, local copies, waits for them, and re-layouts  4.03 us

profile of v1, /device:TPU:1, one launch (start us, length us, event | category | flops | bytes accessed | tf_op | source)
XLA Modules:
  0.0 72.8 jit_solution(8507866446002976142)
XLA Ops:
  0.6 68.2 %shard_map.122 = (bf16[4,64,8192]{2,1,0:T(8,128)(2,1)S(1)}, bf16[8192,256]{1,0:T(8,128)(2,1)S(1)}) custom-call(bf16[4,64,8192]{2,1,0:T(8,128)(2,1)} %x_hbm.1, f32[1,8192]{1,0:T(1,128)} %bitcast.2, bf16[8192,256]{1,0:T(8,128)(2,1)} %wq_hbm.1, bf16[8192,256]{1,0:T(8,128)(2,1)} %wkv_hbm.1, bf16[256,8192]{1,0:T(8,128)(2,1)} %wo_hbm.1, ...), custom_call_target="tpu_custom_call" | custom-call | tf_op jit(solution)/shard_map/pallas_call | solution.py:425
  68.8 2.0 %copy.15 = bf16[4,64,8192]{2,1,0:T(8,128)(2,1)} copy(bf16[4,64,8192]{2,1,0:T(8,128)(2,1)S(1)} %get-tuple-element.2) | data formatting | bytes 8388608
  70.8 2.0 %copy.16 = bf16[8192,256]{1,0:T(8,128)(2,1)} copy(bf16[8192,256]{1,0:T(8,128)(2,1)S(1)} %get-tuple-element.3) | data formatting | bytes 8388608

commit v2 on v1

v2 whole, which is shorter than its diff:
```python
import functools
import math

import jax
import jax.numpy as jnp
from jax import lax
from jax.experimental import pallas as pl
from jax.experimental.pallas import tpu as pltpu
from jax.sharding import PartitionSpec as P

MESH = pl.DeviceIdType.MESH
HD = 128
STEPS = 4
ROWS = 64
HALF = 32
WIDTH = 8192
CHUNK = 1024
NCHUNK = WIDTH // CHUNK
COLS = 4096
CTX = 256
NCOPY = 96
BF = jnp.bfloat16
F32 = jnp.float32


def mult(value, by):
    return pl.multiple_of(value, by)


def kernel(
    x_hbm, gain_hbm, wq_hbm, wkv_hbm, wo_hbm, kv_hbm, len_hbm, dist_hbm, smap_hbm, hold_hbm,
    out, nw,
    gain, len_v, dist, smap,
    xv, w, wo, kv, hold, ordr, w1r, acc, sq, ybf, cs, sn, qs, qr, kn, vn, qf, bias, bias_f,
    pw, pf, mix, att, part, rbx, rb, sb, keep_b, rel_up, rel_dn, dir_o, dir_n, sum_o, sum_n,
    s_up, s_dn, sa, rax, keep_a,
    ld, chunk_sem, hold_sem, ssem, rsem,
):
    dp = lax.axis_index("dp")
    tensor = lax.axis_index("tensor")
    xl, z = dp // 4, lax.rem(dp, 4)
    xh, y, c = tensor // 8, lax.rem(tensor // 2, 4), lax.rem(tensor, 2)

    def dev(xl_, xh_, y_, z_, c_):
        return (xl_ * 4 + z_, xh_ * 8 + y_ * 2 + c_)

    def ring(value, by):
        return lax.rem(value + by + 4, 4)

    copies = []

    def send(src, dst, where):
        i = len(copies)
        cp = pltpu.make_async_remote_copy(
            src_ref=src, dst_ref=dst, send_sem=ssem.at[i], recv_sem=rsem.at[i],
            device_id=where, device_id_type=MESH,
        )
        cp.start()
        copies.append([cp, False])
        return i

    def arrived(i):
        copies[i][0].wait_recv()
        copies[i][1] = True

    sibling = dev(xl, xh, y, z, 1 - c)
    across = dev(xl, 1 - xh, y, z, c)
    cross = dev(1 - xl, 1 - xh, y, z, c)
    near = dev(1 - xl, xh, y, z, c)
    z_up = dev(xl, xh, y, ring(z, 1), c)
    z_down = dev(xl, xh, y, ring(z, -1), c)

    def same_core(k):
        return dev(xl, xh, ring(y, k), z, c)

    barrier = pltpu.get_barrier_semaphore()
    greet = [sibling, across, cross, near, z_up, z_down]
    for k in (1, 2, 3):
        for other in (c, 1 - c):
            greet.append(dev(xl, xh, ring(y, k), z, other))
    for where in greet:
        pl.semaphore_signal(barrier, inc=1, device_id=where, device_id_type=MESH)

    small = [
        pltpu.make_async_copy(a, b, ld.at[i])
        for i, (a, b) in enumerate(
            ((len_hbm, len_v), (gain_hbm, gain), (dist_hbm, dist), (smap_hbm, smap))
        )
    ]
    for cp in small:
        cp.start()

    def chunk_loads(i):
        ks = pl.ds(mult(i * CHUNK, CHUNK), CHUNK)
        return (
            pltpu.make_async_copy(
                x_hbm.at[:, :, :, :, ks], xv.at[:, :, :, :, ks], chunk_sem.at[i, 0]
            ),
            pltpu.make_async_copy(wq_hbm.at[ks], w.at[ks, pl.ds(0, 256)], chunk_sem.at[i, 1]),
            pltpu.make_async_copy(wkv_hbm.at[ks], w.at[ks, pl.ds(256, 256)], chunk_sem.at[i, 2]),
        )

    def start_chunk(i, carry):
        for cp in chunk_loads(i):
            cp.start()
        return carry

    def hold_load(t):
        cols = pl.ds(mult(t * 256, 256), 256)
        return pltpu.make_async_copy(hold_hbm.at[:, :, cols], hold.at[:, t], hold_sem.at[t])

    def start_hold(t, carry):
        hold_load(t).start()
        return carry

    lax.fori_loop(0, 2, start_chunk, 0)
    lax.fori_loop(0, 16, start_hold, 0)
    lax.fori_loop(2, NCHUNK, start_chunk, 0)
    my_half = pl.ds(mult(c * HALF, HALF), HALF)
    load_kv = pltpu.make_async_copy(kv_hbm.at[my_half, 0], kv, ld.at[4])
    load_kv.start()
    my_cols = pl.ds(mult(c * COLS, COLS), COLS)
    sib_cols = pl.ds(mult((1 - c) * COLS, COLS), COLS)
    my_wo = pl.ds(mult(c * 256, 256), 256)
    load_wo = pltpu.make_async_copy(wo_hbm.at[:, my_cols], wo.at[my_wo], ld.at[5])
    load_wo.start()

    acc[...] = jnp.zeros_like(acc)
    sq[...] = jnp.zeros_like(sq)
    for cp in small:
        cp.wait()
    lengths = len_v[...].astype(F32)
    eye = lax.broadcasted_iota(jnp.int32, (ROWS, ROWS), 0) == lax.broadcasted_iota(
        jnp.int32, (ROWS, ROWS), 1
    )
    position = jnp.sum(jnp.where(eye, lengths, 0.0), axis=1, keepdims=True)
    lane = lax.broadcasted_iota(jnp.int32, (1, HD), 1)
    sign = jnp.where(lane < HD // 2, -1.0, 1.0)
    inverse = jnp.exp((lane & (HD // 2 - 1)).astype(F32) * (-math.log(1000000.0) / (HD // 2)))
    for s in range(STEPS):
        angle = (position + float(s)) * inverse
        cs[s] = jnp.cos(angle)
        sn[s] = jnp.sin(angle) * sign

    def mask(b, carry):
        rows = pl.ds(mult(b * 128, 128), 128)
        i = lax.broadcasted_iota(jnp.int32, (128, 1), 0) + b * 128
        r = i >> 4
        step = (i & 7) >> 1
        row_lane = lax.broadcasted_iota(jnp.int32, (1, ROWS), 1)
        limit = jnp.sum(jnp.where(row_lane == r + c * HALF, lengths, 0.0), axis=1, keepdims=True)
        place = lax.broadcasted_iota(jnp.int32, (1, CTX), 1).astype(F32)
        bias[rows, :] = jnp.where(place < limit, 0.0, -jnp.inf)
        n = lax.broadcasted_iota(jnp.int32, (1, 64), 1)
        usable = ((n & 15) == (r & 15)) & ((n >> 4) <= step)
        bias_f[rows, :] = jnp.where(usable, 0.0, -jnp.inf)
        return carry

    lax.fori_loop(0, 4, mask, 0)

    def project(i, carry):
        ks = pl.ds(mult(i * CHUNK, CHUNK), CHUNK)
        for cp in chunk_loads(i):
            cp.wait()
        g = gain[:, ks]
        for s in range(STEPS):
            xs = xv[s, :, :, :, ks].reshape(ROWS, CHUNK).astype(F32)
            ybf[s] = (xs * g).astype(BF)
            xx = xs * xs
            total = xx[:, 0:128]
            for j in range(1, CHUNK // 128):
                total = total + xx[:, j * 128:(j + 1) * 128]
            sq[s] += total
        acc[...] += jnp.dot(
            ybf[...].reshape(STEPS * ROWS, CHUNK), w[ks, :], preferred_element_type=F32
        )
        return carry

    lax.fori_loop(0, 2, project, 0)

    best = dist[0] * 8
    for i in range(1, 8):
        best = jnp.minimum(best, dist[i] * 8 + i)
    chosen = lax.rem(best, 8)

    def hold_done(t, carry):
        hold_load(t).wait()
        return carry

    def order(t, carry):
        ordr[t] = hold[chosen, smap[t]]
        return carry

    lax.fori_loop(0, 16, hold_done, 0)
    lax.fori_loop(0, 16, order, 0)

    pl.semaphore_wait(barrier, len(greet))

    def rows_of(xl_, xh_, y_, z_, c_):
        return pl.ds(mult(((xl_ * 4 + z_) * 16 + xh_ * 8 + y_ * 2 + c_) * 64, 64), 64)

    def slab_of(xl_, xh_, z_):
        return pl.ds(mult(((xl_ * 4 + z_) * 16 + xh_ * 8) * 64, 512), 512)

    mine = rows_of(xl, xh, y, z, c)
    own_copies = []
    for k in (2, 1, 3, 0):
        for flip in (0, 1):
            if k == 0 and flip == 0:
                continue
            yk = ring(y, k)
            ck = (c, 1 - c)[flip]
            own_copies.append(
                send(ordr.at[xh * 8 + yk * 2 + ck], nw.at[mine], dev(xl, xh, yk, z, ck))
            )
    cross_copy = send(ordr.at[pl.ds(mult((1 - xh) * 8, 8), 8)], w1r, cross)
    nw[mine] = ordr[xh * 8 + y * 2 + c]
    wo_copy = send(wo_hbm.at[:, sib_cols], wo.at[my_wo], sibling)

    lax.fori_loop(2, NCHUNK, project, 0)

    def turn(v, s):
        return v * cs[s] + pltpu.roll(v, HD // 2, 1) * sn[s]

    for s in range(STEPS):
        scale = lax.rsqrt(jnp.sum(sq[s], axis=1, keepdims=True) * (1.0 / WIDTH) + 1e-06)
        block = pl.ds(s * ROWS, ROWS)
        for h in range(2):
            cols = slice(h * HD, (h + 1) * HD)
            qs[s, :, cols] = turn(acc[block, cols] * scale, s).astype(BF)
        kn[s] = turn(acc[block, 256:384] * scale, s).astype(BF)
        vn[s] = (acc[block, 384:512] * scale).astype(BF)

    sib_half = pl.ds(mult((1 - c) * HALF, HALF), HALF)
    q_copy = send(qs.at[:, sib_half, :], qr, sibling)
    for s in range(STEPS):
        for h in range(2):
            qf[pl.ds(s * 2 + h, HALF, stride=16), :] = qs[s, my_half, h * HD:(h + 1) * HD].astype(
                F32
            )

    def around(slab):
        return send(nw.at[slab], nw.at[slab], z_up), send(nw.at[slab], nw.at[slab], z_down)

    for i in own_copies:
        arrived(i)
    slab_0a = slab_of(xl, xh, z)
    z_0a = around(slab_0a)
    near_a = send(nw.at[slab_0a], nw.at[slab_0a], near)

    arrived(q_copy)
    for s in range(STEPS):
        for h in range(2):
            qf[pl.ds(8 + s * 2 + h, HALF, stride=16), :] = qr[s, :, h * HD:(h + 1) * HD].astype(F32)
    load_kv.wait()

    factor = 1.0 / math.sqrt(HD)

    def attend(b):
        block = pl.ds(b * 256, 256)
        sub = pl.ds(mult(c * HALF + b * 16, 16), 16)

        def score(i, carry):
            rows = pl.ds(mult(b * 256 + i * 16, 16), 16)
            mine_ = pl.ds(mult(i * 16, 16), 16)
            bias_here = bias[rows, :]
            got = lax.dot_general(
                qf[rows, :].astype(BF), kv[b * 16 + i, :, 0:HD], (((1,), (1,)), ((), ())),
                preferred_element_type=F32,
            )
            bias[rows, :] = got * factor + bias_here
            return carry

        lax.fori_loop(0, 16, score, 0, unroll=8)
        keys = kn[:, sub, :].reshape(STEPS * 16, HD)
        for part_of in range(2):
            rows = pl.ds(b * 256 + part_of * 128, 128)
            fresh = lax.dot_general(
                qf[rows, :].astype(BF), keys, (((1,), (1,)), ((), ())), preferred_element_type=F32
            ) * factor + bias_f[rows, :]
            cached = bias[rows, :]
            top = jnp.maximum(
                jnp.max(cached, axis=1, keepdims=True), jnp.max(fresh, axis=1, keepdims=True)
            )
            ce = jnp.exp(cached - top)
            fe = jnp.exp(fresh - top)
            total = jnp.sum(ce, axis=1, keepdims=True) + jnp.sum(fe, axis=1, keepdims=True)
            share = 1.0 / total
            pw[rows, :] = (ce * share).astype(BF)
            pf[rows, :] = (fe * share).astype(BF)
        values = vn[:, sub, :].reshape(STEPS * 16, HD)
        mix[block, :] = jnp.dot(pf[block, :], values, preferred_element_type=F32)

        def weigh(i, carry):
            rows = pl.ds(mult(b * 256 + i * 16, 16), 16)
            mix[rows, :] += jnp.dot(
                pw[rows, :], kv[b * 16 + i, :, HD:2 * HD], preferred_element_type=F32
            )
            return carry

        lax.fori_loop(0, 16, weigh, 0, unroll=8)
        for source in range(2):
            for s in range(STEPS):
                for h in range(2):
                    base = (c if source == 0 else 1 - c) * 256 + h * HD
                    att[b, s, c, :, pl.ds(mult(base, HD), HD)] = mix[
                        pl.ds(b * 256 + source * 8 + s * 2 + h, 16, stride=16), :
                    ].astype(BF)
        return send(att.at[b, :, c], att.at[b, :, c], sibling)

    def block_cols(yk, side):
        return pl.ds(mult(yk * 1024 + side * 512, 512), 512)

    def term(b, yk, side):
        cols = block_cols(yk, side)
        part[b, :, cols] = jnp.dot(
            att[b].reshape(128, 512), wo[:, cols], preferred_element_type=F32
        ).astype(BF)
        return part.at[b, :, cols]

    up, down, far = ring(y, 1), ring(y, -1), ring(y, 2)
    to_up, to_down = same_core(1), same_core(-1)

    att_b = attend(0)

    arrived(cross_copy)
    theirs = rows_of(1 - xl, 1 - xh, y, z, c)
    cross_copies = []
    for k in (2, 1, 3, 0):
        for flip in (0, 1):
            if k == 0 and flip == 0:
                continue
            yk = ring(y, k)
            ck = (c, 1 - c)[flip]
            cross_copies.append(
                send(w1r.at[yk * 2 + ck], nw.at[theirs], dev(xl, xh, yk, z, ck))
            )
    nw[theirs] = w1r[y * 2 + c]

    load_wo.wait()
    arrived(wo_copy)
    arrived(att_b)
    b_copies, b2 = {}, {}
    for k in (2, 1, 3, 0):
        b_copies[k] = send(term(0, ring(y, k), 1 - xh), rbx.at[k], across)
    for k in (2, 1, 3, 0):
        term(0, ring(y, k), xh)

    att_a = attend(1)

    for i in cross_copies:
        arrived(i)
    slab_0b = slab_of(1 - xl, 1 - xh, z)
    z_0b = around(slab_0b)
    near_b = send(nw.at[slab_0b], nw.at[slab_0b], near)

    arrived(att_a)
    r_up = send(term(1, far, 1 - xh), rel_up, to_up)
    r_dn = send(term(1, far, xh), rel_dn, to_down)
    d_dn = send(term(1, down, 1 - xh), dir_o, to_down)
    d_up = send(term(1, up, xh), dir_n, to_up)
    term(1, up, 1 - xh)
    term(1, down, xh)
    term(1, y, 1 - xh)
    term(1, y, xh)

    def pass_on(k):
        arrived(b_copies[k])
        cols = block_cols(ring(y, k), xh)
        sb[k - 1] = (part[0, :, cols].astype(F32) + rbx[k].astype(F32)).astype(BF)
        b2[k] = send(sb.at[k - 1], rb.at[k - 1], same_core(k))

    pass_on(2)
    arrived(near_a)
    slab_1a = slab_of(1 - xl, xh, z)
    slab_1b = slab_of(xl, 1 - xh, z)
    z_1a = around(slab_1a)
    pass_on(1)
    arrived(r_up)
    s_up[...] = (part[1, :, block_cols(up, 1 - xh)].astype(F32) + rel_up[...].astype(F32)).astype(BF)
    t_up = send(s_up, sum_o, to_up)
    arrived(r_dn)
    s_dn[...] = (part[1, :, block_cols(down, xh)].astype(F32) + rel_dn[...].astype(F32)).astype(BF)
    t_dn = send(s_dn, sum_n, to_down)
    pass_on(3)

    def onward(i, slab, where):
        arrived(i)
        return send(nw.at[slab], nw.at[slab], where)

    onward(z_0a[0], slab_of(xl, xh, ring(z, -1)), z_up)
    arrived(near_b)
    z_1b = around(slab_1b)
    arrived(b_copies[0])
    keep_b[...] = part[0, :, block_cols(y, xh)].astype(F32) + rbx[0].astype(F32)
    onward(z_0b[1], slab_of(1 - xl, 1 - xh, ring(z, 1)), z_down)

    arrived(d_dn)
    arrived(t_up)
    sa[...] = (
        part[1, :, block_cols(y, 1 - xh)].astype(F32)
        + dir_o[...].astype(F32)
        + sum_o[...].astype(F32)
    ).astype(BF)
    a2 = send(sa, rax, across)
    arrived(d_up)
    arrived(t_dn)
    keep_a[...] = (
        part[1, :, block_cols(y, xh)].astype(F32)
        + dir_n[...].astype(F32)
        + sum_n[...].astype(F32)
    )

    def chunk_at(c_, y_, xh_, off=0, size=512):
        return pl.ds(mult(c_ * COLS + y_ * 1024 + xh_ * 512 + off, 128), size)

    def give(b, cols, *wheres):
        ref = out.at[:, :, b, :, cols]
        return [send(ref, ref, where) for where in wheres]

    def finish(b, total):
        cols = chunk_at(c, y, xh)
        whole = xv[:, :, b, :, cols].astype(F32) + total.reshape(STEPS, 2, 16, 512)
        out[:, :, b, :, cols] = whole.astype(BF)

    own = chunk_at(c, y, xh)
    other = chunk_at(c, y, 1 - xh)
    for k in (1, 3, 2):
        arrived(b2[k])
    finish(0, keep_b[...] + rb[0].astype(F32) + rb[1].astype(F32) + rb[2].astype(F32))
    gb_far, gb_up, gb_dn, gb_x = give(0, own, same_core(2), to_up, to_down, across)
    give(0, own, sibling)
    arrived(a2)
    finish(1, keep_a[...] + rax[...].astype(F32))
    ga_x, ga_up, ga_dn = give(1, own, across, to_up, to_down)
    give(1, own, sibling)

    onward(z_1a[0], slab_of(1 - xl, xh, ring(z, -1)), z_up)
    onward(z_1b[1], slab_of(xl, 1 - xh, ring(z, 1)), z_down)

    last = []

    def to_across(i, yk):
        arrived(i)
        cols = chunk_at(c, yk, xh)
        (j,) = give(0, cols, across)
        last.append((j, 0, chunk_at(c, yk, 1 - xh)))
        give(0, cols, sibling)

    def relay(i_up, i_dn, side):
        arrived(i_up)
        (first,) = give(1, chunk_at(c, down, side, 0, 256), to_up)
        arrived(i_dn)
        (second,) = give(1, chunk_at(c, up, side, 256, 256), to_down)
        give(1, chunk_at(c, down, side), sibling)
        give(1, chunk_at(c, up, side), sibling)
        return first, second

    to_across(gb_up, down)
    to_across(gb_dn, up)
    to_across(gb_far, far)
    arrived(gb_x)
    give(0, other, sibling)
    arrived(ga_x)
    oa_up, oa_dn = give(1, other, to_up, to_down)
    give(1, other, sibling)
    near_1, near_2 = relay(ga_up, ga_dn, xh)
    far_1, far_2 = relay(oa_up, oa_dn, 1 - xh)
    for i in (near_1, near_2):
        arrived(i)
    give(1, chunk_at(c, far, xh), sibling)
    for i, b, cols in last:
        arrived(i)
        give(b, cols, sibling)
    for i in (far_1, far_2):
        arrived(i)
    give(1, chunk_at(c, far, 1 - xh), sibling)

    for cp, done in copies:
        if not done:
            cp.wait_recv()
        cp.wait_send()


def on_device(
    inputs, norm_gain, w_query, w_kv, w_out, kv_cache, kv_lengths, reuse_dist, shard_map,
    holder_weights,
):
    hbm = pl.BlockSpec(memory_space=pltpu.HBM)
    vmem = pl.BlockSpec(memory_space=pltpu.VMEM)
    dma = pltpu.SemaphoreType.DMA
    block = (128, 512)
    outputs, next_weights = pl.pallas_call(
        kernel,
        out_shape=(
            pltpu.VMEM((STEPS, 2, 2, 16, WIDTH), BF),
            pltpu.VMEM((WIDTH, 256), BF),
        ),
        in_specs=[hbm] * 10,
        out_specs=(vmem, vmem),
        scratch_shapes=[
            pltpu.VMEM((1, WIDTH), F32),
            pltpu.VMEM((1, ROWS), jnp.int32),
            pltpu.SMEM((8,), jnp.int32),
            pltpu.SMEM((16,), jnp.int32),
            pltpu.VMEM((STEPS, 2, 2, 16, WIDTH), BF),
            pltpu.VMEM((WIDTH, 512), BF),
            pltpu.VMEM((512, COLS), BF),
            pltpu.VMEM((HALF, CTX, 2 * HD), BF),
            pltpu.VMEM((8, 16, 64, 256), BF),
            pltpu.VMEM((16, 64, 256), BF),
            pltpu.VMEM((8, 64, 256), BF),
            pltpu.VMEM((STEPS * ROWS, 512), F32),
            pltpu.VMEM((STEPS, ROWS, 128), F32),
            pltpu.VMEM((STEPS, ROWS, CHUNK), BF),
            pltpu.VMEM((STEPS, ROWS, HD), F32),
            pltpu.VMEM((STEPS, ROWS, HD), F32),
            pltpu.VMEM((STEPS, ROWS, 256), BF),
            pltpu.VMEM((STEPS, HALF, 256), BF),
            pltpu.VMEM((STEPS, ROWS, HD), BF),
            pltpu.VMEM((STEPS, ROWS, HD), BF),
            pltpu.VMEM((512, HD), F32),
            pltpu.VMEM((512, CTX), F32),
            pltpu.VMEM((512, 64), F32),
            pltpu.VMEM((512, CTX), BF),
            pltpu.VMEM((512, 64), BF),
            pltpu.VMEM((512, HD), F32),
            pltpu.VMEM((2, STEPS, 2, 16, 512), BF),
            pltpu.VMEM((2, 128, COLS), BF),
            pltpu.VMEM((4,) + block, BF),
            pltpu.VMEM((3,) + block, BF),
            pltpu.VMEM((3,) + block, BF),
            pltpu.VMEM(block, F32),
            pltpu.VMEM(block, BF),
            pltpu.VMEM(block, BF),
            pltpu.VMEM(block, BF),
            pltpu.VMEM(block, BF),
            pltpu.VMEM(block, BF),
            pltpu.VMEM(block, BF),
            pltpu.VMEM(block, BF),
            pltpu.VMEM(block, BF),
            pltpu.VMEM(block, BF),
            pltpu.VMEM(block, BF),
            pltpu.VMEM(block, F32),
            dma((6,)),
            dma((NCHUNK, 3)),
            dma((16,)),
            dma((NCOPY,)),
            dma((NCOPY,)),
        ],
        compiler_params=pltpu.CompilerParams(
            collective_id=0, has_side_effects=True, vmem_limit_bytes=48 * 1024 * 1024
        ),
    )(
        inputs.reshape(STEPS, 2, 2, 16, WIDTH), norm_gain.reshape(1, WIDTH), w_query, w_kv, w_out,
        kv_cache, kv_lengths.reshape(1, ROWS), reuse_dist, shard_map, holder_weights,
    )
    return outputs.reshape(STEPS, ROWS, WIDTH), next_weights


def solution(mesh):
    in_specs = (
        P(None, "dp", None),
        P(),
        P(None, "tensor"),
        P(None, "tensor"),
        P("tensor", None),
        P("dp", "tensor", None, None),
        P("dp"),
        P(),
        P(),
        P(None, ("dp", "tensor"), None),
    )
    out_specs = (P(None, "dp", None), P(None, "tensor"))
    return jax.shard_map(
        on_device, mesh=mesh, in_specs=in_specs, out_specs=out_specs, check_vma=False
    )
```

time: 73 us -> 65.3 us (0.89)
  Pallas kernels: 68.2 us -> 60.5 us
    pallas_call x1, Pallas kernels: 68.2 us -> 60.5 us  [on_device(): pl.pallas_call(kernel, out_shape=(pltpu.VMEM((STEPS, 2, 2, 16, WIDTH), BF...]
where the time goes in v2:
time: 65.3 us; the launch traced here: 65.2 us
  Pallas kernels  60.5 us (93%)
  local copies, waits for them, and re-layouts  4.03 us (6%)
    pallas_call x1, Pallas kernels, on_device(): pl.pallas_call(kernel, out_shape=(pltpu.VMEM((STEPS, 2, 2, 16, WIDTH), BF...  60.5 us
    unnamed x2, local copies, waits for them, and re-layouts  4.03 us

profile of v2, /device:TPU:1, one launch (start us, length us, event | category | flops | bytes accessed | tf_op | source)
XLA Modules:
  0.0 65.2 jit_solution(18326902173352780072)
XLA Ops:
  0.6 60.5 %shard_map.113 = (bf16[4,2,2,16,8192]{4,3,2,1,0:T(8,128)(2,1)S(1)}, bf16[8192,256]{1,0:T(8,128)(2,1)S(1)}) custom-call(bf16[4,2,2,16,8192]{4,3,2,1,0:T(8,128)(2,1)} %bitcast.5, f32[1,8192]{1,0:T(1,128)} %bitcast.6, bf16[8192,256]{1,0:T(8,128)(2,1)} %wq_hbm.1, bf16[8192,256]{1,0:T(8,128)(2,1)} %wkv_hbm.1, bf16[256,8192]{1,0:T(8,128)(2,1)} %wo_hbm.1, ...), custom_call_target="tpu_custom_call" | custom-call | tf_op jit(solution)/shard_map/pallas_call | solution.py:493
  61.1 2.0 %copy.14 = bf16[4,64,8192]{2,1,0:T(8,128)(2,1)} copy(bf16[4,64,8192]{2,1,0:T(8,128)(2,1)S(1)} %bitcast.4) | data formatting | bytes 8388608
  63.1 2.0 %copy.15 = bf16[8192,256]{1,0:T(8,128)(2,1)} copy(bf16[8192,256]{1,0:T(8,128)(2,1)S(1)} %get-tuple-element.7) | data formatting | bytes 8388608

commit v3 on v2

--- a/solution.py
+++ b/solution.py
@@ -18,7 +18,7 @@
 NCHUNK = WIDTH // CHUNK
 COLS = 4096
 CTX = 256
-NCOPY = 96
+NCOPY = 84
 BF = jnp.bfloat16
 F32 = jnp.float32
 
@@ -34,7 +34,7 @@
     xv, w, wo, kv, hold, ordr, w1r, acc, sq, ybf, cs, sn, qs, qr, kn, vn, qf, bias, bias_f,
     pw, pf, mix, att, part, rbx, rb, sb, keep_b, rel_up, rel_dn, dir_o, dir_n, sum_o, sum_n,
     s_up, s_dn, sa, rax, keep_a,
-    ld, chunk_sem, hold_sem, ssem, rsem,
+    ld, chunk_sem, ssem, rsem,
 ):
     dp = lax.axis_index("dp")
     tensor = lax.axis_index("tensor")
@@ -47,21 +47,31 @@
     def ring(value, by):
         return lax.rem(value + by + 4, 4)
 
-    copies = []
-
-    def send(src, dst, where):
-        i = len(copies)
-        cp = pltpu.make_async_remote_copy(
-            src_ref=src, dst_ref=dst, send_sem=ssem.at[i], recv_sem=rsem.at[i],
+    used, sent, pending = [], [0, 0, 0, 0], {}
+
+    def flag():
+        used.append(0)
+        return len(used) - 1
+
+    def kib(ref):
+        return math.prod(ref.shape) * 2 // 1024
+
+    def send(src, dst, where, group=None, lane=0):
+        i = flag() if group is None else group
+        pltpu.make_async_remote_copy(
+            src_ref=src, dst_ref=dst, send_sem=ssem.at[lane], recv_sem=rsem.at[i],
             device_id=where, device_id_type=MESH,
-        )
-        cp.start()
-        copies.append([cp, False])
+        ).start()
+        sent[lane] += kib(src)
+        pending[i] = pending.get(i, 0) + kib(dst)
         return i
 
+    def wait_kib(sem, amount):
+        ref = w.at[pl.ds(0, amount)]
+        pltpu.make_async_copy(ref, ref, sem).wait()
+
     def arrived(i):
-        copies[i][0].wait_recv()
-        copies[i][1] = True
+        wait_kib(rsem.at[i], pending.pop(i))
 
     sibling = dev(xl, xh, y, z, 1 - c)
     across = dev(xl, 1 - xh, y, z, c)
@@ -97,7 +107,7 @@
                 x_hbm.at[:, :, :, :, ks], xv.at[:, :, :, :, ks], chunk_sem.at[i, 0]
             ),
             pltpu.make_async_copy(wq_hbm.at[ks], w.at[ks, pl.ds(0, 256)], chunk_sem.at[i, 1]),
-            pltpu.make_async_copy(wkv_hbm.at[ks], w.at[ks, pl.ds(256, 256)], chunk_sem.at[i, 2]),
+            pltpu.make_async_copy(wkv_hbm.at[ks], w.at[ks, pl.ds(256, 256)], chunk_sem.at[i, 1]),
         )
 
     def start_chunk(i, carry):
@@ -105,12 +115,14 @@
             cp.start()
         return carry
 
-    def hold_load(t):
+    def wait_chunk(i):
+        ks = pl.ds(mult(i * CHUNK, CHUNK), CHUNK)
+        chunk_loads(i)[0].wait()
+        pltpu.make_async_copy(w.at[ks], w.at[ks], chunk_sem.at[i, 1]).wait()
+
+    def start_hold(t, carry):
         cols = pl.ds(mult(t * 256, 256), 256)
-        return pltpu.make_async_copy(hold_hbm.at[:, :, cols], hold.at[:, t], hold_sem.at[t])
-
-    def start_hold(t, carry):
-        hold_load(t).start()
+        pltpu.make_async_copy(hold_hbm.at[:, :, cols], hold.at[:, t], ld.at[6]).start()
         return carry
 
     lax.fori_loop(0, 2, start_chunk, 0)
@@ -160,8 +172,7 @@
 
     def project(i, carry):
         ks = pl.ds(mult(i * CHUNK, CHUNK), CHUNK)
-        for cp in chunk_loads(i):
-            cp.wait()
+        wait_chunk(i)
         g = gain[:, ks]
         for s in range(STEPS):
             xs = xv[s, :, :, :, ks].reshape(ROWS, CHUNK).astype(F32)
@@ -183,15 +194,11 @@
         best = jnp.minimum(best, dist[i] * 8 + i)
     chosen = lax.rem(best, 8)
 
-    def hold_done(t, carry):
-        hold_load(t).wait()
-        return carry
-
     def order(t, carry):
         ordr[t] = hold[chosen, smap[t]]
         return carry
 
-    lax.fori_loop(0, 16, hold_done, 0)
+    pltpu.make_async_copy(hold, hold, ld.at[6]).wait()
     lax.fori_loop(0, 16, order, 0)
 
     pl.semaphore_wait(barrier, len(greet))
@@ -199,25 +206,78 @@
     def rows_of(xl_, xh_, y_, z_, c_):
         return pl.ds(mult(((xl_ * 4 + z_) * 16 + xh_ * 8 + y_ * 2 + c_) * 64, 64), 64)
 
-    def slab_of(xl_, xh_, z_):
-        return pl.ds(mult(((xl_ * 4 + z_) * 16 + xh_ * 8) * 64, 512), 512)
+    def to_ranks(source, rows, order_):
+        groups = {}
+        for k in order_:
+            yk = ring(y, k)
+            groups[k] = flag()
+            for flip in (0, 1):
+                if k or flip:
+                    ck = (c, 1 - c)[flip]
+                    send(source.at[yk * 2 + ck], nw.at[rows], dev(xl, xh, yk, z, ck), groups[k])
+        return groups
 
     mine = rows_of(xl, xh, y, z, c)
-    own_copies = []
+    own_copies = to_ranks(ordr.at[pl.ds(mult(xh * 8, 8), 8)], mine, (0, 1, 3, 2))
+    cross_copies = {}
     for k in (2, 1, 3, 0):
-        for flip in (0, 1):
-            if k == 0 and flip == 0:
-                continue
-            yk = ring(y, k)
-            ck = (c, 1 - c)[flip]
-            own_copies.append(
-                send(ordr.at[xh * 8 + yk * 2 + ck], nw.at[mine], dev(xl, xh, yk, z, ck))
-            )
-    cross_copy = send(ordr.at[pl.ds(mult((1 - xh) * 8, 8), 8)], w1r, cross)
+        cross_copies[k] = send(
+            ordr.at[pl.ds((1 - xh) * 8 + ring(y, k) * 2, 2)],
+            w1r.at[pl.ds(ring(y, k) * 2, 2)],
+            cross,
+        )
     nw[mine] = ordr[xh * 8 + y * 2 + c]
     wo_copy = send(wo_hbm.at[:, sib_cols], wo.at[my_wo], sibling)
 
-    lax.fori_loop(2, NCHUNK, project, 0)
+    lax.fori_loop(2, 6, project, 0)
+
+    def pair_of(xl_, xh_, k):
+        return pl.ds(mult(((xl_ * 4 + z) * 16 + xh_ * 8 + ring(y, -k) * 2) * 64, 128), 128)
+
+    slabs = {"0a": (xl, xh), "0b": (1 - xl, 1 - xh), "1a": (1 - xl, xh), "1b": (xl, 1 - xh)}
+    z_groups = {name: (flag(), flag()) for name in slabs}
+    last_z = flag()
+    near_copies = {"a": {}, "b": {}}
+
+    def around(name, k):
+        ref = nw.at[pair_of(*slabs[name], k)]
+        send(ref, ref, z_up, z_groups[name][0])
+        send(ref, ref, z_down, z_groups[name][1])
+        if name[0] == "0":
+            near_copies[name[1]][k] = send(ref, ref, near)
+
+    def onward(name):
+        xl_, xh_ = slabs[name]
+        arrived(z_groups[name][0])
+        low = nw.at[pl.ds(mult(((xl_ * 4 + ring(z, -1)) * 16 + xh_ * 8) * 64, 256), 256)]
+        send(low, low, z_up, last_z)
+        arrived(z_groups[name][1])
+        high = nw.at[pl.ds(mult(((xl_ * 4 + ring(z, 1)) * 16 + xh_ * 8) * 64 + 256, 256), 256)]
+        send(high, high, z_down, last_z)
+
+    theirs = rows_of(1 - xl, 1 - xh, y, z, c)
+    theirs_copies = {}
+
+    def serve_theirs(k):
+        arrived(cross_copies[k])
+        if k == 0:
+            nw[theirs] = w1r[y * 2 + c]
+        theirs_copies.update(to_ranks(w1r, theirs, (k,)))
+
+    def first_around(k):
+        arrived(own_copies[k])
+        around("0a", k)
+
+    def second_around(k):
+        arrived(theirs_copies[k])
+        around("0b", k)
+
+    def near_around(part_, k):
+        arrived(near_copies[part_][k])
+        around("1" + part_, k)
+
+    lax.fori_loop(6, NCHUNK, project, 0)
+    first_around(0)
 
     def turn(v, s):
         return v * cs[s] + pltpu.roll(v, HD // 2, 1) * sn[s]
@@ -239,15 +299,8 @@
                 F32
             )
 
-    def around(slab):
-        return send(nw.at[slab], nw.at[slab], z_up), send(nw.at[slab], nw.at[slab], z_down)
-
-    for i in own_copies:
-        arrived(i)
-    slab_0a = slab_of(xl, xh, z)
-    z_0a = around(slab_0a)
-    near_a = send(nw.at[slab_0a], nw.at[slab_0a], near)
-
+    for k in (1, 3, 2):
+        first_around(k)
     arrived(q_copy)
     for s in range(STEPS):
         for h in range(2):
@@ -316,127 +369,189 @@
         part[b, :, cols] = jnp.dot(
             att[b].reshape(128, 512), wo[:, cols], preferred_element_type=F32
         ).astype(BF)
-        return part.at[b, :, cols]
+
+    def piece(u, yk, side):
+        return part.at[u // 2, pl.ds(u % 2 * 64, 64), block_cols(yk, side)]
 
     up, down, far = ring(y, 1), ring(y, -1), ring(y, 2)
-    to_up, to_down = same_core(1), same_core(-1)
-
-    att_b = attend(0)
-
-    arrived(cross_copy)
-    theirs = rows_of(1 - xl, 1 - xh, y, z, c)
-    cross_copies = []
-    for k in (2, 1, 3, 0):
-        for flip in (0, 1):
-            if k == 0 and flip == 0:
-                continue
-            yk = ring(y, k)
-            ck = (c, 1 - c)[flip]
-            cross_copies.append(
-                send(w1r.at[yk * 2 + ck], nw.at[theirs], dev(xl, xh, yk, z, ck))
-            )
-    nw[theirs] = w1r[y * 2 + c]
+    to_up, to_down, to_far = same_core(1), same_core(-1), same_core(2)
+    o, n = 1 - xh, xh
+
+    att_0 = attend(0)
+
+    serve_theirs(2)
+    serve_theirs(1)
 
     load_wo.wait()
     arrived(wo_copy)
-    arrived(att_b)
-    b_copies, b2 = {}, {}
-    for k in (2, 1, 3, 0):
-        b_copies[k] = send(term(0, ring(y, k), 1 - xh), rbx.at[k], across)
-    for k in (2, 1, 3, 0):
-        term(0, ring(y, k), xh)
-
-    att_a = attend(1)
-
-    for i in cross_copies:
-        arrived(i)
-    slab_0b = slab_of(1 - xl, 1 - xh, z)
-    z_0b = around(slab_0b)
-    near_b = send(nw.at[slab_0b], nw.at[slab_0b], near)
-
-    arrived(att_a)
-    r_up = send(term(1, far, 1 - xh), rel_up, to_up)
-    r_dn = send(term(1, far, xh), rel_dn, to_down)
-    d_dn = send(term(1, down, 1 - xh), dir_o, to_down)
-    d_up = send(term(1, up, xh), dir_n, to_up)
-    term(1, up, 1 - xh)
-    term(1, down, xh)
-    term(1, y, 1 - xh)
-    term(1, y, xh)
+    arrived(att_0)
+    relay_up, relay_dn, direct_o, direct_n, a_across = {}, {}, {}, {}, {}
+    b_copies, b2 = {}, flag()
+
+    def start_relays(u):
+        relay_up[u] = send(piece(u, far, o), rel_up.at[u - 1], to_up, lane=3)
+        relay_dn[u] = send(piece(u, far, n), rel_dn.at[u - 1], to_down, lane=3)
+
+    def start_direct(u):
+        direct_o[u], direct_n[u] = flag(), flag()
+        send(piece(u, down, o), dir_o.at[u - 1], to_down, direct_o[u], 3)
+        send(piece(u, up, n), dir_n.at[u - 1], to_up, direct_n[u], 3)
+
+    def start_b(k):
+        b_copies[k] = send(piece(0, ring(y, k), o), rbx.at[k], across, lane=3)
+
+    term(0, far, o)
+    term(0, far, n)
+    start_relays(1)
+    start_b(2)
+    term(0, down, o)
+    term(0, up, n)
+    start_direct(1)
+    start_b(3)
+    term(0, up, o)
+    start_b(1)
+    term(0, y, o)
+    start_b(0)
+    term(0, down, n)
+    term(0, y, n)
+
+    att_1 = attend(1)
+
+    serve_theirs(3)
+    serve_theirs(0)
+    near_around("a", 0)
+
+    def relay_sums(u):
+        arrived(relay_up[u])
+        s_up[u - 1] = (
+            piece(u, up, o)[...].astype(F32) + rel_up[u - 1].astype(F32)
+        ).astype(BF)
+        send(s_up.at[u - 1], sum_o.at[u - 1], to_up, direct_o[u], 3)
+        arrived(relay_dn[u])
+        s_dn[u - 1] = (
+            piece(u, down, n)[...].astype(F32) + rel_dn[u - 1].astype(F32)
+        ).astype(BF)
+        send(s_dn.at[u - 1], sum_n.at[u - 1], to_down, direct_n[u], 3)
+
+    relay_sums(1)
+    arrived(att_1)
+    term(1, far, o)
+    term(1, far, n)
+    start_relays(2)
+    start_relays(3)
+    term(1, down, o)
+    term(1, up, n)
+    start_direct(2)
+    start_direct(3)
+    term(1, up, o)
+    term(1, down, n)
+    term(1, y, o)
+    term(1, y, n)
 
     def pass_on(k):
         arrived(b_copies[k])
-        cols = block_cols(ring(y, k), xh)
-        sb[k - 1] = (part[0, :, cols].astype(F32) + rbx[k].astype(F32)).astype(BF)
-        b2[k] = send(sb.at[k - 1], rb.at[k - 1], same_core(k))
+        sb[k - 1] = (
+            piece(0, ring(y, k), n)[...].astype(F32) + rbx[k].astype(F32)
+        ).astype(BF)
+        send(sb.at[k - 1], rb.at[k - 1], same_core(k), b2, 3)
+
+    def own_sums(u):
+        arrived(direct_o[u])
+        sa[u - 1] = (
+            piece(u, y, o)[...].astype(F32)
+            + dir_o[u - 1].astype(F32)
+            + sum_o[u - 1].astype(F32)
+        ).astype(BF)
+        a_across[u] = send(sa.at[u - 1], rax.at[u - 1], across, lane=3)
+        arrived(direct_n[u])
+        keep_a[u - 1] = (
+            piece(u, y, n)[...].astype(F32)
+            + dir_n[u - 1].astype(F32)
+            + sum_n[u - 1].astype(F32)
+        )
 
     pass_on(2)
-    arrived(near_a)
-    slab_1a = slab_of(1 - xl, xh, z)
-    slab_1b = slab_of(xl, 1 - xh, z)
-    z_1a = around(slab_1a)
+    second_around(2)
+    second_around(1)
+    near_around("a", 1)
+    near_around("a", 3)
+    near_around("a", 2)
+    pass_on(3)
+    second_around(3)
+    second_around(0)
     pass_on(1)
-    arrived(r_up)
-    s_up[...] = (part[1, :, block_cols(up, 1 - xh)].astype(F32) + rel_up[...].astype(F32)).astype(BF)
-    t_up = send(s_up, sum_o, to_up)
-    arrived(r_dn)
-    s_dn[...] = (part[1, :, block_cols(down, xh)].astype(F32) + rel_dn[...].astype(F32)).astype(BF)
-    t_dn = send(s_dn, sum_n, to_down)
-    pass_on(3)
-
-    def onward(i, slab, where):
-        arrived(i)
-        return send(nw.at[slab], nw.at[slab], where)
-
-    onward(z_0a[0], slab_of(xl, xh, ring(z, -1)), z_up)
-    arrived(near_b)
-    z_1b = around(slab_1b)
+    own_sums(1)
+    relay_sums(2)
     arrived(b_copies[0])
-    keep_b[...] = part[0, :, block_cols(y, xh)].astype(F32) + rbx[0].astype(F32)
-    onward(z_0b[1], slab_of(1 - xl, 1 - xh, ring(z, 1)), z_down)
-
-    arrived(d_dn)
-    arrived(t_up)
-    sa[...] = (
-        part[1, :, block_cols(y, 1 - xh)].astype(F32)
-        + dir_o[...].astype(F32)
-        + sum_o[...].astype(F32)
-    ).astype(BF)
-    a2 = send(sa, rax, across)
-    arrived(d_up)
-    arrived(t_dn)
-    keep_a[...] = (
-        part[1, :, block_cols(y, xh)].astype(F32)
-        + dir_n[...].astype(F32)
-        + sum_n[...].astype(F32)
-    )
+    keep_b[...] = piece(0, y, n)[...].astype(F32) + rbx[0].astype(F32)
+    relay_sums(3)
+    onward("0a")
 
     def chunk_at(c_, y_, xh_, off=0, size=512):
         return pl.ds(mult(c_ * COLS + y_ * 1024 + xh_ * 512 + off, 128), size)
 
-    def give(b, cols, *wheres):
-        ref = out.at[:, :, b, :, cols]
-        return [send(ref, ref, where) for where in wheres]
-
-    def finish(b, total):
+    def give(u, cols, *wheres):
+        ref = out.at[pl.ds(u % 2 * 2, 2), :, u // 2, :, cols]
+        return [send(ref, ref, where, lane=1) for where in wheres]
+
+    to_sibling = flag()
+
+    def share(u, cols):
+        ref = out.at[pl.ds(u % 2 * 2, 2), :, u // 2, :, cols]
+        send(ref, ref, sibling, to_sibling, 2)
+
+    def finish(u, total):
         cols = chunk_at(c, y, xh)
-        whole = xv[:, :, b, :, cols].astype(F32) + total.reshape(STEPS, 2, 16, 512)
-        out[:, :, b, :, cols] = whole.astype(BF)
+        steps = pl.ds(u % 2 * 2, 2)
+        whole = xv[steps, :, u // 2, :, cols].astype(F32) + total.reshape(2, 2, 16, 512)
+        out[steps, :, u // 2, :, cols] = whole.astype(BF)
 
     own = chunk_at(c, y, xh)
     other = chunk_at(c, y, 1 - xh)
-    for k in (1, 3, 2):
-        arrived(b2[k])
+    ga, oa, near_parts, far_parts = {}, {}, {}, {}
+
+    def finish_a(u):
+        arrived(a_across[u])
+        finish(u, keep_a[u - 1] + rax[u - 1].astype(F32))
+        ga[u] = give(u, own, across, to_up, to_down)
+        share(u, own)
+
+    def other_block(u):
+        arrived(ga[u][0])
+        oa[u] = give(u, other, to_up, to_down)
+        share(u, other)
+
+    def relay(u, i_up, i_dn, side):
+        group = flag()
+        arrived(i_up)
+        ref = out.at[pl.ds(u % 2 * 2, 2), :, u // 2, :, chunk_at(c, down, side, 0, 256)]
+        send(ref, ref, to_up, group, 1)
+        arrived(i_dn)
+        ref = out.at[pl.ds(u % 2 * 2, 2), :, u // 2, :, chunk_at(c, up, side, 256, 256)]
+        send(ref, ref, to_down, group, 1)
+        share(u, chunk_at(c, down, side))
+        share(u, chunk_at(c, up, side))
+        return group
+
+    def last_of(u, group, side):
+        arrived(group)
+        share(u, chunk_at(c, far, side))
+
+    own_sums(2)
+    finish_a(1)
+    own_sums(3)
+    for k in (2, 1, 3, 0):
+        near_around("b", k)
+    arrived(b2)
     finish(0, keep_b[...] + rb[0].astype(F32) + rb[1].astype(F32) + rb[2].astype(F32))
-    gb_far, gb_up, gb_dn, gb_x = give(0, own, same_core(2), to_up, to_down, across)
-    give(0, own, sibling)
-    arrived(a2)
-    finish(1, keep_a[...] + rax[...].astype(F32))
-    ga_x, ga_up, ga_dn = give(1, own, across, to_up, to_down)
-    give(1, own, sibling)
-
-    onward(z_1a[0], slab_of(1 - xl, xh, ring(z, -1)), z_up)
-    onward(z_1b[1], slab_of(xl, 1 - xh, ring(z, 1)), z_down)
+    gb_far, gb_up, gb_dn, gb_x = give(0, own, to_far, to_up, to_down, across)
+    share(0, own)
+    finish_a(2)
+    near_parts[1] = relay(1, ga[1][1], ga[1][2], xh)
+    other_block(1)
+    finish_a(3)
+    onward("0b")
+    onward("1a")
 
     last = []
 
@@ -444,42 +559,48 @@
         arrived(i)
         cols = chunk_at(c, yk, xh)
         (j,) = give(0, cols, across)
-        last.append((j, 0, chunk_at(c, yk, 1 - xh)))
-        give(0, cols, sibling)
-
-    def relay(i_up, i_dn, side):
-        arrived(i_up)
-        (first,) = give(1, chunk_at(c, down, side, 0, 256), to_up)
-        arrived(i_dn)
-        (second,) = give(1, chunk_at(c, up, side, 256, 256), to_down)
-        give(1, chunk_at(c, down, side), sibling)
-        give(1, chunk_at(c, up, side), sibling)
-        return first, second
+        last.append((j, chunk_at(c, yk, 1 - xh)))
+        share(0, cols)
 
     to_across(gb_up, down)
     to_across(gb_dn, up)
+    near_parts[2] = relay(2, ga[2][1], ga[2][2], xh)
+    other_block(2)
     to_across(gb_far, far)
+    near_parts[3] = relay(3, ga[3][1], ga[3][2], xh)
+    other_block(3)
+    far_parts[1] = relay(1, oa[1][0], oa[1][1], 1 - xh)
+    onward("1b")
     arrived(gb_x)
-    give(0, other, sibling)
-    arrived(ga_x)
-    oa_up, oa_dn = give(1, other, to_up, to_down)
-    give(1, other, sibling)
-    near_1, near_2 = relay(ga_up, ga_dn, xh)
-    far_1, far_2 = relay(oa_up, oa_dn, 1 - xh)
-    for i in (near_1, near_2):
+    share(0, other)
+    last_of(1, near_parts[1], xh)
+    far_parts[2] = relay(2, oa[2][0], oa[2][1], 1 - xh)
+    last_of(2, near_parts[2], xh)
+    far_parts[3] = relay(3, oa[3][0], oa[3][1], 1 - xh)
+    last_of(1, far_parts[1], 1 - xh)
+    last_of(3, near_parts[3], xh)
+    for i, cols in last:
         arrived(i)
-    give(1, chunk_at(c, far, xh), sibling)
-    for i, b, cols in last:
+        share(0, cols)
+    last_of(2, far_parts[2], 1 - xh)
+    last_of(3, far_parts[3], 1 - xh)
+
+    assert len(used) <= NCOPY
+    for i in list(pending):
         arrived(i)
-        give(b, cols, sibling)
-    for i in (far_1, far_2):
-        arrived(i)
-    give(1, chunk_at(c, far, 1 - xh), sibling)
-
-    for cp, done in copies:
-        if not done:
-            cp.wait_recv()
-        cp.wait_send()
+    for lane_, amount in enumerate(sent):
+        wait_kib(ssem.at[lane_], amount)
+
+
+def store(out_ref, nw_ref, out_hbm, nw_hbm, sem):
+    copies = [
+        pltpu.make_async_copy(out_ref, out_hbm, sem.at[0]),
+        pltpu.make_async_copy(nw_ref, nw_hbm, sem.at[1]),
+    ]
+    for cp in copies:
+        cp.start()
+    for cp in copies:
+        cp.wait()
 
 
 def on_device(
@@ -489,7 +610,7 @@
     hbm = pl.BlockSpec(memory_space=pltpu.HBM)
     vmem = pl.BlockSpec(memory_space=pltpu.VMEM)
     dma = pltpu.SemaphoreType.DMA
-    block = (128, 512)
+    block = (64, 512)
     outputs, next_weights = pl.pallas_call(
         kernel,
         out_shape=(
@@ -531,21 +652,20 @@
             pltpu.VMEM((3,) + block, BF),
             pltpu.VMEM((3,) + block, BF),
             pltpu.VMEM(block, F32),
-            pltpu.VMEM(block, BF),
-            pltpu.VMEM(block, BF),
-            pltpu.VMEM(block, BF),
-            pltpu.VMEM(block, BF),
-            pltpu.VMEM(block, BF),
-            pltpu.VMEM(block, BF),
-            pltpu.VMEM(block, BF),
-            pltpu.VMEM(block, BF),
-            pltpu.VMEM(block, BF),
-            pltpu.VMEM(block, BF),
-            pltpu.VMEM(block, F32),
-            dma((6,)),
-            dma((NCHUNK, 3)),
-            dma((16,)),
-            dma((NCOPY,)),
+            pltpu.VMEM((3,) + block, BF),
+            pltpu.VMEM((3,) + block, BF),
+            pltpu.VMEM((3,) + block, BF),
+            pltpu.VMEM((3,) + block, BF),
+            pltpu.VMEM((3,) + block, BF),
+            pltpu.VMEM((3,) + block, BF),
+            pltpu.VMEM((3,) + block, BF),
+            pltpu.VMEM((3,) + block, BF),
+            pltpu.VMEM((3,) + block, BF),
+            pltpu.VMEM((3,) + block, BF),
+            pltpu.VMEM((3,) + block, F32),
+            dma((7,)),
+            dma((NCHUNK, 2)),
+            dma((4,)),
             dma((NCOPY,)),
         ],
         compiler_params=pltpu.CompilerParams(
@@ -554,6 +674,20 @@
     )(
         inputs.reshape(STEPS, 2, 2, 16, WIDTH), norm_gain.reshape(1, WIDTH), w_query, w_kv, w_out,
         kv_cache, kv_lengths.reshape(1, ROWS), reuse_dist, shard_map, holder_weights,
+    )
+    outputs, next_weights = pl.pallas_call(
+        store,
+        out_shape=(
+            pltpu.HBM((STEPS, 2, 2, 16, WIDTH), BF),
+            pltpu.HBM((WIDTH, 256), BF),
+        ),
+        in_specs=[vmem, vmem],
+        out_specs=(hbm, hbm),
+        scratch_shapes=[dma((2,))],
+        compiler_params=pltpu.CompilerParams(vmem_limit_bytes=4 * 1024 * 1024),
+    )(
+        pltpu.with_memory_space_constraint(outputs, pltpu.VMEM),
+        pltpu.with_memory_space_constraint(next_weights, pltpu.VMEM),
     )
     return outputs.reshape(STEPS, ROWS, WIDTH), next_weights
 

time: 65.3 us -> 59.2 us (0.907)
  local copies, waits for them, and re-layouts: 4.03 us -> 0 us
  Pallas kernels: 60.5 us -> 58.5 us
    pallas_call x1, Pallas kernels: 60.5 us -> 55.1 us  [on_device(): pl.pallas_call(kernel, out_shape=(pltpu.VMEM((STEPS, 2, 2, 16, WIDTH), BF...]
    unnamed x2 -> x0, local copies, waits for them, and re-layouts: 4.03 us -> none
    pallas_call x0 -> x1, Pallas kernels: none -> 3.41 us  [on_device(): pl.pallas_call(store, out_shape=(pltpu.HBM((STEPS, 2, 2, 16, WIDTH), BF),...]
where the time goes in v3:
time: 59.2 us; the launch traced here: 59.1 us
  Pallas kernels  58.5 us (99%)
  between operations  0.64 us (1%)
    pallas_call x1, Pallas kernels, on_device(): pl.pallas_call(kernel, out_shape=(pltpu.VMEM((STEPS, 2, 2, 16, WIDTH), BF...  55.1 us
    pallas_call x1, Pallas kernels, on_device(): pl.pallas_call(store, out_shape=(pltpu.HBM((STEPS, 2, 2, 16, WIDTH), BF),...  3.41 us

profile of v3, /device:TPU:1, one launch (start us, length us, event | category | flops | bytes accessed | tf_op | source)
XLA Modules:
  0.0 59.1 jit_solution(8547641314362378932)
XLA Ops:
  0.6 55.1 %shard_map.113 = (bf16[4,2,2,16,8192]{4,3,2,1,0:T(8,128)(2,1)S(1)}, bf16[8192,256]{1,0:T(8,128)(2,1)S(1)}) custom-call(bf16[4,2,2,16,8192]{4,3,2,1,0:T(8,128)(2,1)} %bitcast.4, f32[1,8192]{1,0:T(1,128)} %bitcast.5, bf16[8192,256]{1,0:T(8,128)(2,1)} %wq_hbm.1, bf16[8192,256]{1,0:T(8,128)(2,1)} %wkv_hbm.1, bf16[256,8192]{1,0:T(8,128)(2,1)} %wo_hbm.1, ...), custom_call_target="tpu_custom_call" | custom-call | tf_op jit(solution)/shard_map/pallas_call | solution.py:614
  55.7 3.4 %shard_map.114 = (bf16[4,2,2,16,8192]{4,3,2,1,0:T(8,128)(2,1)}, bf16[8192,256]{1,0:T(8,128)(2,1)}) custom-call(bf16[4,2,2,16,8192]{4,3,2,1,0:T(8,128)(2,1)S(1)} %get-tuple-element.6.out_ref, bf16[8192,256]{1,0:T(8,128)(2,1)S(1)} %get-tuple-element.7.nw_ref), custom_call_target="tpu_custom_call" | custom-call | tf_op jit(solution)/shard_map/pallas_call | solution.py:678

commit v4 on v3

--- a/solution.py
+++ b/solution.py
@@ -18,7 +18,27 @@
 NCHUNK = WIDTH // CHUNK
 COLS = 4096
 CTX = 256
-NCOPY = 84
+NCOPY = 96
+GROUPS = (
+    (0, 0, 2, "A"),
+    (0, 2, 2, "Br"),
+    (1, 0, 2, "A"),
+    (1, 2, 1, "A"),
+    (1, 3, 1, "B"),
+)
+ORDER = (
+    "W.f1", "W.f3", "attend0", "W.f2", "W.s2", "W.s1", "W.a0", "attend1", "g1.bf", "g1.bd",
+    "g0.relay", "g0.direct", "g1.bo", "g2.relay", "g4.bf", "g4.bd", "g4.bo", "g4.bu", "g3.relay",
+    "g1.bu", "g3.direct", "W.s0", "g2.direct", "W.a1", "W.s3", "W.q2", "W.a3", "W.q1", "W.q0",
+    "g0.sumd", "g0.sumu", "g1.pf", "g2.sumu", "g1.po", "g2.sumd", "g3.sumd", "g4.pf", "g3.sumu",
+    "g4.pd", "g4.po", "W.o0a", "g4.pu", "W.q3", "g0.o", "g1.pu", "W.b2", "g0.n", "g1.pd", "g2.o",
+    "W.a2", "g2.n", "g3.o", "W.b1", "g3.n", "W.b0", "g4.fin", "W.b3", "W.o0b", "g1.fin",
+    "g0.fino", "W.o1a", "g0.finn", "g4.af", "g4.ad", "g4.au", "g2.fino", "g1.ad", "g1.au",
+    "g2.finn", "g3.fino", "W.o1b", "g0.rod", "g3.finn", "g0.rou", "g4.lx", "g0.rnu", "g0.rnd",
+    "g1.lx", "g2.rod", "g2.rou", "g4.lf", "g1.af", "g4.ld", "g4.lu", "g2.rnu", "g2.rnd", "g3.rou",
+    "g1.ld", "g3.rod", "g3.rnu", "g3.rnd", "g0.lo", "g1.lu", "g0.ln", "g2.lo", "g1.lf", "g2.ln",
+    "g3.lo", "g3.ln",
+)
 BF = jnp.bfloat16
 F32 = jnp.float32
 
@@ -32,8 +52,8 @@
     out, nw,
     gain, len_v, dist, smap,
     xv, w, wo, kv, hold, ordr, w1r, acc, sq, ybf, cs, sn, qs, qr, kn, vn, qf, bias, bias_f,
-    pw, pf, mix, att, part, rbx, rb, sb, keep_b, rel_up, rel_dn, dir_o, dir_n, sum_o, sum_n,
-    s_up, s_dn, sa, rax, keep_a,
+    pw, pf, mix, att, part, rbx, rb, sb, rel_up, rel_dn, dir_o, dir_n, sum_o, sum_n,
+    s_up, s_dn, sa, rax, rbh, keep,
     ld, chunk_sem, ssem, rsem,
 ):
     dp = lax.axis_index("dp")
@@ -100,25 +120,25 @@
     for cp in small:
         cp.start()
 
-    def chunk_loads(i):
+    def load_x(i):
         ks = pl.ds(mult(i * CHUNK, CHUNK), CHUNK)
-        return (
-            pltpu.make_async_copy(
-                x_hbm.at[:, :, :, :, ks], xv.at[:, :, :, :, ks], chunk_sem.at[i, 0]
-            ),
-            pltpu.make_async_copy(wq_hbm.at[ks], w.at[ks, pl.ds(0, 256)], chunk_sem.at[i, 1]),
-            pltpu.make_async_copy(wkv_hbm.at[ks], w.at[ks, pl.ds(256, 256)], chunk_sem.at[i, 1]),
+        return pltpu.make_async_copy(
+            x_hbm.at[:, :, :, :, ks], xv.at[:, :, :, :, ks], chunk_sem.at[i, 0]
         )
 
+    def load_wq(i):
+        ks = pl.ds(mult(i * CHUNK, CHUNK), CHUNK)
+        return pltpu.make_async_copy(wq_hbm.at[ks], w.at[ks, pl.ds(0, 256)], chunk_sem.at[i, 1])
+
+    def load_wkv(i):
+        ks = pl.ds(mult(i * CHUNK, CHUNK), CHUNK)
+        return pltpu.make_async_copy(wkv_hbm.at[ks], w.at[ks, pl.ds(256, 256)], chunk_sem.at[i, 2])
+
     def start_chunk(i, carry):
-        for cp in chunk_loads(i):
-            cp.start()
+        load_x(i).start()
+        load_wq(i).start()
+        load_wkv(i).start()
         return carry
-
-    def wait_chunk(i):
-        ks = pl.ds(mult(i * CHUNK, CHUNK), CHUNK)
-        chunk_loads(i)[0].wait()
-        pltpu.make_async_copy(w.at[ks], w.at[ks], chunk_sem.at[i, 1]).wait()
 
     def start_hold(t, carry):
         cols = pl.ds(mult(t * 256, 256), 256)
@@ -172,7 +192,9 @@
 
     def project(i, carry):
         ks = pl.ds(mult(i * CHUNK, CHUNK), CHUNK)
-        wait_chunk(i)
+        load_x(i).wait()
+        load_wq(i).wait()
+        load_wkv(i).wait()
         g = gain[:, ks]
         for s in range(STEPS):
             xs = xv[s, :, :, :, ks].reshape(ROWS, CHUNK).astype(F32)
@@ -276,8 +298,8 @@
         arrived(near_copies[part_][k])
         around("1" + part_, k)
 
+    first_around(0)
     lax.fori_loop(6, NCHUNK, project, 0)
-    first_around(0)
 
     def turn(v, s):
         return v * cs[s] + pltpu.roll(v, HD // 2, 1) * sn[s]
@@ -288,24 +310,20 @@
         for h in range(2):
             cols = slice(h * HD, (h + 1) * HD)
             qs[s, :, cols] = turn(acc[block, cols] * scale, s).astype(BF)
+        if s == STEPS - 1:
+            sib_half = pl.ds(mult((1 - c) * HALF, HALF), HALF)
+            q_copy = send(qs.at[:, sib_half, :], qr, sibling)
+    for s in range(STEPS):
+        scale = lax.rsqrt(jnp.sum(sq[s], axis=1, keepdims=True) * (1.0 / WIDTH) + 1e-06)
+        block = pl.ds(s * ROWS, ROWS)
         kn[s] = turn(acc[block, 256:384] * scale, s).astype(BF)
         vn[s] = (acc[block, 384:512] * scale).astype(BF)
 
-    sib_half = pl.ds(mult((1 - c) * HALF, HALF), HALF)
-    q_copy = send(qs.at[:, sib_half, :], qr, sibling)
     for s in range(STEPS):
         for h in range(2):
             qf[pl.ds(s * 2 + h, HALF, stride=16), :] = qs[s, my_half, h * HD:(h + 1) * HD].astype(
                 F32
             )
-
-    for k in (1, 3, 2):
-        first_around(k)
-    arrived(q_copy)
-    for s in range(STEPS):
-        for h in range(2):
-            qf[pl.ds(8 + s * 2 + h, HALF, stride=16), :] = qr[s, :, h * HD:(h + 1) * HD].astype(F32)
-    load_kv.wait()
 
     factor = 1.0 / math.sqrt(HD)
 
@@ -370,220 +388,252 @@
             att[b].reshape(128, 512), wo[:, cols], preferred_element_type=F32
         ).astype(BF)
 
-    def piece(u, yk, side):
-        return part.at[u // 2, pl.ds(u % 2 * 64, 64), block_cols(yk, side)]
-
     up, down, far = ring(y, 1), ring(y, -1), ring(y, 2)
     to_up, to_down, to_far = same_core(1), same_core(-1), same_core(2)
     o, n = 1 - xh, xh
 
-    att_0 = attend(0)
-
-    serve_theirs(2)
-    serve_theirs(1)
-
-    load_wo.wait()
-    arrived(wo_copy)
-    arrived(att_0)
-    relay_up, relay_dn, direct_o, direct_n, a_across = {}, {}, {}, {}, {}
-    b_copies, b2 = {}, flag()
-
-    def start_relays(u):
-        relay_up[u] = send(piece(u, far, o), rel_up.at[u - 1], to_up, lane=3)
-        relay_dn[u] = send(piece(u, far, n), rel_dn.at[u - 1], to_down, lane=3)
-
-    def start_direct(u):
-        direct_o[u], direct_n[u] = flag(), flag()
-        send(piece(u, down, o), dir_o.at[u - 1], to_down, direct_o[u], 3)
-        send(piece(u, up, n), dir_n.at[u - 1], to_up, direct_n[u], 3)
-
-    def start_b(k):
-        b_copies[k] = send(piece(0, ring(y, k), o), rbx.at[k], across, lane=3)
-
-    term(0, far, o)
-    term(0, far, n)
-    start_relays(1)
-    start_b(2)
-    term(0, down, o)
-    term(0, up, n)
-    start_direct(1)
-    start_b(3)
-    term(0, up, o)
-    start_b(1)
-    term(0, y, o)
-    start_b(0)
-    term(0, down, n)
-    term(0, y, n)
-
-    att_1 = attend(1)
-
-    serve_theirs(3)
-    serve_theirs(0)
-    near_around("a", 0)
-
-    def relay_sums(u):
-        arrived(relay_up[u])
-        s_up[u - 1] = (
-            piece(u, up, o)[...].astype(F32) + rel_up[u - 1].astype(F32)
-        ).astype(BF)
-        send(s_up.at[u - 1], sum_o.at[u - 1], to_up, direct_o[u], 3)
-        arrived(relay_dn[u])
-        s_dn[u - 1] = (
-            piece(u, down, n)[...].astype(F32) + rel_dn[u - 1].astype(F32)
-        ).astype(BF)
-        send(s_dn.at[u - 1], sum_n.at[u - 1], to_down, direct_n[u], 3)
-
-    relay_sums(1)
-    arrived(att_1)
-    term(1, far, o)
-    term(1, far, n)
-    start_relays(2)
-    start_relays(3)
-    term(1, down, o)
-    term(1, up, n)
-    start_direct(2)
-    start_direct(3)
-    term(1, up, o)
-    term(1, down, n)
-    term(1, y, o)
-    term(1, y, n)
-
-    def pass_on(k):
-        arrived(b_copies[k])
-        sb[k - 1] = (
-            piece(0, ring(y, k), n)[...].astype(F32) + rbx[k].astype(F32)
-        ).astype(BF)
-        send(sb.at[k - 1], rb.at[k - 1], same_core(k), b2, 3)
-
-    def own_sums(u):
-        arrived(direct_o[u])
-        sa[u - 1] = (
-            piece(u, y, o)[...].astype(F32)
-            + dir_o[u - 1].astype(F32)
-            + sum_o[u - 1].astype(F32)
-        ).astype(BF)
-        a_across[u] = send(sa.at[u - 1], rax.at[u - 1], across, lane=3)
-        arrived(direct_n[u])
-        keep_a[u - 1] = (
-            piece(u, y, n)[...].astype(F32)
-            + dir_n[u - 1].astype(F32)
-            + sum_n[u - 1].astype(F32)
-        )
-
-    pass_on(2)
-    second_around(2)
-    second_around(1)
-    near_around("a", 1)
-    near_around("a", 3)
-    near_around("a", 2)
-    pass_on(3)
-    second_around(3)
-    second_around(0)
-    pass_on(1)
-    own_sums(1)
-    relay_sums(2)
-    arrived(b_copies[0])
-    keep_b[...] = piece(0, y, n)[...].astype(F32) + rbx[0].astype(F32)
-    relay_sums(3)
-    onward("0a")
+
+    tasks = {}
+    for k in range(4):
+        tasks[f"W.s{k}"] = functools.partial(serve_theirs, k)
+        tasks[f"W.q{k}"] = functools.partial(second_around, k)
+        tasks[f"W.a{k}"] = functools.partial(near_around, "a", k)
+        tasks[f"W.b{k}"] = functools.partial(near_around, "b", k)
+    for name in slabs:
+        tasks["W.o" + name] = functools.partial(onward, name)
+
+    att_copies = {}
+
+    def attend_to(b):
+        if b == 0:
+            arrived(q_copy)
+            for s in range(STEPS):
+                for h in range(2):
+                    qf[pl.ds(8 + s * 2 + h, HALF, stride=16), :] = qr[
+                        s, :, h * HD:(h + 1) * HD
+                    ].astype(F32)
+            load_kv.wait()
+        att_copies[b] = attend(b)
+
+    for b in range(2):
+        tasks[f"attend{b}"] = functools.partial(attend_to, b)
+    for k in (1, 2, 3):
+        tasks[f"W.f{k}"] = functools.partial(first_around, k)
+    made, ready = set(), set()
+
+    def need(b, *blocks):
+        if not ready:
+            load_wo.wait()
+            arrived(wo_copy)
+        if b not in ready:
+            ready.add(b)
+            arrived(att_copies[b])
+        for name, yk, side in blocks:
+            if (b, name) not in made:
+                made.add((b, name))
+                term(b, yk, side)
+
+    block_of = {
+        "fo": (far, o), "fn": (far, n), "uo": (up, o), "un": (up, n),
+        "do": (down, o), "dn": (down, n), "o": (y, o), "n": (y, n),
+    }
+    to_sibling = flag()
 
     def chunk_at(c_, y_, xh_, off=0, size=512):
         return pl.ds(mult(c_ * COLS + y_ * 1024 + xh_ * 512 + off, 128), size)
 
-    def give(u, cols, *wheres):
-        ref = out.at[pl.ds(u % 2 * 2, 2), :, u // 2, :, cols]
-        return [send(ref, ref, where, lane=1) for where in wheres]
-
-    to_sibling = flag()
-
-    def share(u, cols):
-        ref = out.at[pl.ds(u % 2 * 2, 2), :, u // 2, :, cols]
-        send(ref, ref, sibling, to_sibling, 2)
-
-    def finish(u, total):
-        cols = chunk_at(c, y, xh)
-        steps = pl.ds(u % 2 * 2, 2)
-        whole = xv[steps, :, u // 2, :, cols].astype(F32) + total.reshape(2, 2, 16, 512)
-        out[steps, :, u // 2, :, cols] = whole.astype(BF)
-
     own = chunk_at(c, y, xh)
     other = chunk_at(c, y, 1 - xh)
-    ga, oa, near_parts, far_parts = {}, {}, {}, {}
-
-    def finish_a(u):
-        arrived(a_across[u])
-        finish(u, keep_a[u - 1] + rax[u - 1].astype(F32))
-        ga[u] = give(u, own, across, to_up, to_down)
-        share(u, own)
-
-    def other_block(u):
-        arrived(ga[u][0])
-        oa[u] = give(u, other, to_up, to_down)
-        share(u, other)
-
-    def relay(u, i_up, i_dn, side):
-        group = flag()
-        arrived(i_up)
-        ref = out.at[pl.ds(u % 2 * 2, 2), :, u // 2, :, chunk_at(c, down, side, 0, 256)]
-        send(ref, ref, to_up, group, 1)
-        arrived(i_dn)
-        ref = out.at[pl.ds(u % 2 * 2, 2), :, u // 2, :, chunk_at(c, up, side, 256, 256)]
-        send(ref, ref, to_down, group, 1)
-        share(u, chunk_at(c, down, side))
-        share(u, chunk_at(c, up, side))
-        return group
-
-    def last_of(u, group, side):
-        arrived(group)
-        share(u, chunk_at(c, far, side))
-
-    own_sums(2)
-    finish_a(1)
-    own_sums(3)
-    for k in (2, 1, 3, 0):
-        near_around("b", k)
-    arrived(b2)
-    finish(0, keep_b[...] + rb[0].astype(F32) + rb[1].astype(F32) + rb[2].astype(F32))
-    gb_far, gb_up, gb_dn, gb_x = give(0, own, to_far, to_up, to_down, across)
-    share(0, own)
-    finish_a(2)
-    near_parts[1] = relay(1, ga[1][1], ga[1][2], xh)
-    other_block(1)
-    finish_a(3)
-    onward("0b")
-    onward("1a")
-
-    last = []
-
-    def to_across(i, yk):
-        arrived(i)
-        cols = chunk_at(c, yk, xh)
-        (j,) = give(0, cols, across)
-        last.append((j, chunk_at(c, yk, 1 - xh)))
-        share(0, cols)
-
-    to_across(gb_up, down)
-    to_across(gb_dn, up)
-    near_parts[2] = relay(2, ga[2][1], ga[2][2], xh)
-    other_block(2)
-    to_across(gb_far, far)
-    near_parts[3] = relay(3, ga[3][1], ga[3][2], xh)
-    other_block(3)
-    far_parts[1] = relay(1, oa[1][0], oa[1][1], 1 - xh)
-    onward("1b")
-    arrived(gb_x)
-    share(0, other)
-    last_of(1, near_parts[1], xh)
-    far_parts[2] = relay(2, oa[2][0], oa[2][1], 1 - xh)
-    last_of(2, near_parts[2], xh)
-    far_parts[3] = relay(3, oa[3][0], oa[3][1], 1 - xh)
-    last_of(1, far_parts[1], 1 - xh)
-    last_of(3, near_parts[3], xh)
-    for i, cols in last:
-        arrived(i)
-        share(0, cols)
-    last_of(2, far_parts[2], 1 - xh)
-    last_of(3, far_parts[3], 1 - xh)
+
+    def add_group(g, b, step, steps, kind):
+        rows = steps * 32
+        span = pl.ds(step * 32, rows)
+        f = {}
+
+        def slot(ref, *index):
+            return ref.at[(g,) + index + (pl.ds(0, rows),)]
+
+        def mine_of(name):
+            need(b, (name,) + block_of[name])
+            return part.at[b, span, block_cols(*block_of[name])]
+
+        def wide(ref):
+            return ref[...].astype(F32)
+
+        def out_at(cols):
+            return out.at[pl.ds(step, steps), :, b, :, cols]
+
+        def give(cols, where, group=None):
+            return send(out_at(cols), out_at(cols), where, group, 1)
+
+        def share(cols):
+            send(out_at(cols), out_at(cols), sibling, to_sibling, 2)
+
+        def finish(total, cols):
+            ref = xv.at[pl.ds(step, steps), :, b, :, cols]
+            out_at(cols)[...] = (wide(ref) + total.reshape(steps, 2, 16, 512)).astype(BF)
+
+        def add(name, run):
+            tasks[f"g{g}.{name}"] = run
+
+        def relay():
+            f["ru"] = send(mine_of("fo"), slot(rel_up), to_up, lane=3)
+            f["rd"] = send(mine_of("fn"), slot(rel_dn), to_down, lane=3)
+
+        def direct():
+            f["o"], f["n"] = flag(), flag()
+            send(mine_of("do"), slot(dir_o), to_down, f["o"], 3)
+            send(mine_of("un"), slot(dir_n), to_up, f["n"], 3)
+
+        def sum_up():
+            first = wide(mine_of("uo"))
+            arrived(f["ru"])
+            slot(s_up)[...] = (first + wide(slot(rel_up))).astype(BF)
+            send(slot(s_up), slot(sum_o), to_up, f["o"], 3)
+
+        def sum_down():
+            first = wide(mine_of("dn"))
+            arrived(f["rd"])
+            slot(s_dn)[...] = (first + wide(slot(rel_dn))).astype(BF)
+            send(slot(s_dn), slot(sum_n), to_down, f["n"], 3)
+
+        def own_sum(q, more, added):
+            first = wide(mine_of(q))
+            arrived(f[q])
+            slot(sa, "no".index(q))[...] = (first + wide(more) + wide(added)).astype(BF)
+            ref = slot(sa, "no".index(q))
+            f["x" + q] = send(ref, slot(rax, "on".index(q)), across, lane=3)
+
+        def finish_a(q, cols):
+            arrived(f["x" + ("o" if q == "n" else "n")])
+            i = "no".index(q)
+            finish(wide(slot(sa, i)) + wide(slot(rax, i)), cols)
+            f["gu" + q] = give(cols, to_up)
+            f["gd" + q] = give(cols, to_down)
+            share(cols)
+
+        def half_up(q, side):
+            arrived(f["gu" + q])
+            if "h" + q not in f:
+                f["h" + q] = flag()
+            give(chunk_at(c, down, side, 0, 256), to_up, f["h" + q])
+            share(chunk_at(c, down, side))
+
+        def half_down(q, side):
+            arrived(f["gd" + q])
+            if "h" + q not in f:
+                f["h" + q] = flag()
+            give(chunk_at(c, up, side, 256, 256), to_down, f["h" + q])
+            share(chunk_at(c, up, side))
+
+        def last_far(q, side):
+            arrived(f["h" + q])
+            share(chunk_at(c, far, side))
+
+        to = {"f": (far, to_far), "u": (up, to_up), "d": (down, to_down)}
+
+        def start(k):
+            cols = k + "o" if k in to else "o"
+            f["x" + k] = send(mine_of(cols), slot(rbx, "fudo".index(k)), across, lane=3)
+
+        def pass_on(k):
+            first = wide(mine_of(k + "n"))
+            arrived(f["x" + k])
+            i = "fud".index(k)
+            if "y" not in f:
+                f["y"] = flag()
+            if kind == "Br" and k == "f":
+                slot(sb, i)[...] = (first + wide(slot(rbx, i))).astype(BF)
+                f["hu"] = send(
+                    slot(sb, i).at[:, pl.ds(0, 256)], slot(rbh, 0), to_up, lane=3
+                )
+                f["hd"] = send(
+                    slot(sb, i).at[:, pl.ds(256, 256)], slot(rbh, 1), to_down, lane=3
+                )
+                return
+            total = first + wide(slot(rbx, i))
+            if kind == "Br":
+                arrived(f["h" + k])
+                if k == "u":
+                    more = jnp.concatenate(
+                        [total[:, :256] + wide(slot(rbh, 0)), total[:, 256:]], axis=1
+                    )
+                else:
+                    more = jnp.concatenate(
+                        [total[:, :256], total[:, 256:] + wide(slot(rbh, 1))], axis=1
+                    )
+                total = more
+            slot(sb, i)[...] = total.astype(BF)
+            send(slot(sb, i), slot(rb, i), to[k][1], f["y"], 3)
+
+        def pass_own():
+            first = wide(mine_of("n"))
+            arrived(f["xo"])
+            slot(keep)[...] = first + wide(slot(rbx, 3))
+
+        def finish_b():
+            arrived(f["y"])
+            total = slot(keep)[...] + wide(slot(rb, 1)) + wide(slot(rb, 2))
+            if kind == "B":
+                total = total + wide(slot(rb, 0))
+            finish(total, own)
+            if kind == "B":
+                f["gf"] = give(own, to_far)
+            f["gu"] = give(own, to_up)
+            f["gd"] = give(own, to_down)
+            f["gx"] = give(own, across)
+            share(own)
+
+        source = {"f": far, "u": down, "d": up}
+
+        def to_across(k):
+            arrived(f["g" + k])
+            if kind == "Br" and k != "f":
+                if "gf" not in f:
+                    f["gf"] = flag()
+                if k == "u":
+                    give(chunk_at(c, down, xh, 0, 256), to_up, f["gf"])
+                else:
+                    give(chunk_at(c, up, xh, 256, 256), to_down, f["gf"])
+            f["z" + k] = give(chunk_at(c, source[k], xh), across)
+            share(chunk_at(c, source[k], xh))
+
+        def last_across(k):
+            arrived(f["z" + k])
+            share(chunk_at(c, source[k], 1 - xh))
+
+        def last_own():
+            arrived(f["gx"])
+            share(other)
+
+        if kind == "A":
+            add("relay", relay)
+            add("direct", direct)
+            add("sumu", sum_up)
+            add("sumd", sum_down)
+            add("o", functools.partial(own_sum, "o", slot(dir_o), slot(sum_o)))
+            add("n", functools.partial(own_sum, "n", slot(dir_n), slot(sum_n)))
+            for q, side, cols in (("n", xh, own), ("o", 1 - xh, other)):
+                add("fin" + q, functools.partial(finish_a, q, cols))
+                add(f"r{q}u", functools.partial(half_up, q, side))
+                add(f"r{q}d", functools.partial(half_down, q, side))
+                add("l" + q, functools.partial(last_far, q, side))
+        else:
+            for k in "fudo":
+                add("b" + k, functools.partial(start, k))
+            for k in "fud":
+                add("p" + k, functools.partial(pass_on, k))
+                add("a" + k, functools.partial(to_across, k))
+                add("l" + k, functools.partial(last_across, k))
+            add("po", pass_own)
+            add("fin", finish_b)
+            add("lx", last_own)
+
+    for g, spec in enumerate(GROUPS):
+        add_group(g, *spec)
+    assert sorted(ORDER) == sorted(tasks)
+    for name in ORDER:
+        tasks[name]()
 
     assert len(used) <= NCOPY
     for i in list(pending):
@@ -610,7 +660,7 @@
     hbm = pl.BlockSpec(memory_space=pltpu.HBM)
     vmem = pl.BlockSpec(memory_space=pltpu.VMEM)
     dma = pltpu.SemaphoreType.DMA
-    block = (64, 512)
+    block = (len(GROUPS), 64, 512)
     outputs, next_weights = pl.pallas_call(
         kernel,
         out_shape=(
@@ -648,23 +698,23 @@
             pltpu.VMEM((512, HD), F32),
             pltpu.VMEM((2, STEPS, 2, 16, 512), BF),
             pltpu.VMEM((2, 128, COLS), BF),
-            pltpu.VMEM((4,) + block, BF),
-            pltpu.VMEM((3,) + block, BF),
-            pltpu.VMEM((3,) + block, BF),
+            pltpu.VMEM((len(GROUPS), 4, 64, 512), BF),
+            pltpu.VMEM((len(GROUPS), 3, 64, 512), BF),
+            pltpu.VMEM((len(GROUPS), 3, 64, 512), BF),
+            pltpu.VMEM(block, BF),
+            pltpu.VMEM(block, BF),
+            pltpu.VMEM(block, BF),
+            pltpu.VMEM(block, BF),
+            pltpu.VMEM(block, BF),
+            pltpu.VMEM(block, BF),
+            pltpu.VMEM(block, BF),
+            pltpu.VMEM(block, BF),
+            pltpu.VMEM((len(GROUPS), 2, 64, 512), BF),
+            pltpu.VMEM((len(GROUPS), 2, 64, 512), BF),
+            pltpu.VMEM((len(GROUPS), 2, 64, 256), BF),
             pltpu.VMEM(block, F32),
-            pltpu.VMEM((3,) + block, BF),
-            pltpu.VMEM((3,) + block, BF),
-            pltpu.VMEM((3,) + block, BF),
-            pltpu.VMEM((3,) + block, BF),
-            pltpu.VMEM((3,) + block, BF),
-            pltpu.VMEM((3,) + block, BF),
-            pltpu.VMEM((3,) + block, BF),
-            pltpu.VMEM((3,) + block, BF),
-            pltpu.VMEM((3,) + block, BF),
-            pltpu.VMEM((3,) + block, BF),
-            pltpu.VMEM((3,) + block, F32),
             dma((7,)),
-            dma((NCHUNK, 2)),
+            dma((NCHUNK, 3)),
             dma((4,)),
             dma((NCOPY,)),
         ],

time: 59.2 us -> 56.2 us (0.949)
  Pallas kernels: 58.5 us -> 55.5 us
    pallas_call x1, Pallas kernels: 55.1 us -> 52.1 us  [on_device(): pl.pallas_call(kernel, out_shape=(pltpu.VMEM((STEPS, 2, 2, 16, WIDTH), BF...]
where the time goes in v4:
time: 56.2 us; the launch traced here: 56.1 us
  Pallas kernels  55.5 us (99%)
  between operations  0.64 us (1%)
    pallas_call x1, Pallas kernels, on_device(): pl.pallas_call(kernel, out_shape=(pltpu.VMEM((STEPS, 2, 2, 16, WIDTH), BF...  52.1 us
    pallas_call x1, Pallas kernels, on_device(): pl.pallas_call(store, out_shape=(pltpu.HBM((STEPS, 2, 2, 16, WIDTH), BF),...  3.41 us

profile of v4, /device:TPU:1, one launch (start us, length us, event | category | flops | bytes accessed | tf_op | source)
XLA Modules:
  0.0 56.1 jit_solution(5946171086305912046)
XLA Ops:
  0.6 52.1 %shard_map.113 = (bf16[4,2,2,16,8192]{4,3,2,1,0:T(8,128)(2,1)S(1)}, bf16[8192,256]{1,0:T(8,128)(2,1)S(1)}) custom-call(bf16[4,2,2,16,8192]{4,3,2,1,0:T(8,128)(2,1)} %bitcast.4, f32[1,8192]{1,0:T(1,128)} %bitcast.5, bf16[8192,256]{1,0:T(8,128)(2,1)} %wq_hbm.1, bf16[8192,256]{1,0:T(8,128)(2,1)} %wkv_hbm.1, bf16[256,8192]{1,0:T(8,128)(2,1)} %wo_hbm.1, ...), custom_call_target="tpu_custom_call" | custom-call | tf_op jit(solution)/shard_map/pallas_call | solution.py:664
  52.7 3.4 %shard_map.114 = (bf16[4,2,2,16,8192]{4,3,2,1,0:T(8,128)(2,1)}, bf16[8192,256]{1,0:T(8,128)(2,1)}) custom-call(bf16[4,2,2,16,8192]{4,3,2,1,0:T(8,128)(2,1)S(1)} %get-tuple-element.6.out_ref, bf16[8192,256]{1,0:T(8,128)(2,1)S(1)} %get-tuple-element.7.nw_ref), custom_call_target="tpu_custom_call" | custom-call | tf_op jit(solution)/shard_map/pallas_call | solution.py:728

commit v5 on v4

--- a/solution.py
+++ b/solution.py
@@ -104,10 +104,11 @@
         return dev(xl, xh, ring(y, k), z, c)
 
     barrier = pltpu.get_barrier_semaphore()
-    greet = [sibling, across, cross, near, z_up, z_down]
-    for k in (1, 2, 3):
-        for other in (c, 1 - c):
+    greet = [across]
+    for k in (2, 1, 3):
+        for other in (1 - c, c):
             greet.append(dev(xl, xh, ring(y, k), z, other))
+    greet += [z_up, z_down, cross, near, sibling]
     for where in greet:
         pl.semaphore_signal(barrier, inc=1, device_id=where, device_id_type=MESH)
 

time: 56.2 us -> 56.3 us (level)
  no operation moved by 1% of the time
where the time goes in v5:
time: 56.3 us; the launch traced here: 56.2 us
  Pallas kernels  55.5 us (99%)
  between operations  0.64 us (1%)
    pallas_call x1, Pallas kernels, on_device(): pl.pallas_call(kernel, out_shape=(pltpu.VMEM((STEPS, 2, 2, 16, WIDTH), BF...  52.1 us
    pallas_call x1, Pallas kernels, on_device(): pl.pallas_call(store, out_shape=(pltpu.HBM((STEPS, 2, 2, 16, WIDTH), BF),...  3.41 us

profile of v5, /device:TPU:1, one launch (start us, length us, event | category | flops | bytes accessed | tf_op | source)
XLA Modules:
  0.0 56.2 jit_solution(11342026837262711052)
XLA Ops:
  0.6 52.1 %shard_map.113 = (bf16[4,2,2,16,8192]{4,3,2,1,0:T(8,128)(2,1)S(1)}, bf16[8192,256]{1,0:T(8,128)(2,1)S(1)}) custom-call(bf16[4,2,2,16,8192]{4,3,2,1,0:T(8,128)(2,1)} %bitcast.4, f32[1,8192]{1,0:T(1,128)} %bitcast.5, bf16[8192,256]{1,0:T(8,128)(2,1)} %wq_hbm.1, bf16[8192,256]{1,0:T(8,128)(2,1)} %wkv_hbm.1, bf16[256,8192]{1,0:T(8,128)(2,1)} %wo_hbm.1, ...), custom_call_target="tpu_custom_call" | custom-call | tf_op jit(solution)/shard_map/pallas_call | solution.py:665
  52.7 3.4 %shard_map.114 = (bf16[4,2,2,16,8192]{4,3,2,1,0:T(8,128)(2,1)}, bf16[8192,256]{1,0:T(8,128)(2,1)}) custom-call(bf16[4,2,2,16,8192]{4,3,2,1,0:T(8,128)(2,1)S(1)} %get-tuple-element.6.out_ref, bf16[8192,256]{1,0:T(8,128)(2,1)S(1)} %get-tuple-element.7.nw_ref), custom_call_target="tpu_custom_call" | custom-call | tf_op jit(solution)/shard_map/pallas_call | solution.py:729
